TPU v7x, 256 devices: a whole 4x4x8 slice. The times are simulated.
256 devices in a mesh: dp: 8 (over z), mrow: 8 (over y_lo, x), mcol: 4 (over y_hi, core).
Axes of the slice: x: 4, y: 4 (y_hi: 2, y_lo: 2; y = y_hi * 2 + y_lo), z: 8, core: 2. Of those that a mesh axis runs over, the one named last changes fastest.
Arguments:
- weight: float32 [18432, 12288], P(('mrow', 'dp'), 'mcol'), may hold values from -8 to 8
- activations: bfloat16 [1536, 18432], P('dp', 'mrow'), may hold values from -80 to 80
- cotangent: bfloat16 [1536, 12288], P('dp', 'mcol'), may hold values from -10 to 10
- row_old: float32 [18432], replicated, may hold values from 0.1 to 1000
- col_old: float32 [12288], replicated, may hold values from 0.1 to 10
- next_input: bfloat16 [1536, 18432], P('dp', 'mrow'), may hold values from -6 to 6
Outputs:
- new_weight: float32 [18432, 12288], P(('mrow', 'dp'), 'mcol')
- row_factor: float32 [18432], P(('mrow', 'dp'))
- col_factor: float32 [12288], P('mcol')
- queries: float32 [1536, 12288], P(('dp', 'mrow'), 'mcol')
- scaled_step: float32 [18432, 12288], P(('mrow', 'dp'), 'mcol')
All inputs are finite; a program needn't handle non-finite values.
Results may differ from a plain program's by a relative error of at most 0.0029.
Values may be sent and summed in bfloat16 or wider, within the bound.
A program may use at most 128 MiB of HBM per device.

v0:
```python
import jax
import jax.numpy as jnp
from jax import lax
from jax.sharding import PartitionSpec as P

SECOND_DECAY = 1.0 - 10.0 ** (-0.8)
SQUARE_EPS = 1e-30
STEP_RATE = 0.01


def body(weight, activations, cotangent, row_old, col_old, next_input):
    shard_rows = weight.shape[0]
    shard_cols = weight.shape[1]
    width_all = row_old.shape[0]
    outputs_all = col_old.shape[0]
    row_base = (lax.axis_index("mrow") * lax.axis_size("dp") + lax.axis_index("dp")) * shard_rows
    col_base = lax.axis_index("mcol") * shard_cols
    inputs = activations
    grad = lax.psum_scatter(
        lax.dot_general(
            inputs, cotangent, (((0,), (0,)), ((), ())), preferred_element_type=jnp.float32
        ),
        "dp",
        scatter_dimension=0,
        tiled=True,
    )
    squares = grad * grad
    row_part = jnp.sum(squares, axis=1)
    col_part = jnp.sum(squares, axis=0)
    vector = jnp.zeros((width_all + outputs_all,), jnp.float32)
    vector = lax.dynamic_update_slice(vector, row_part, (row_base,))
    vector = lax.dynamic_update_slice(vector, col_part, (width_all + col_base,))
    summed = lax.psum(vector, ("dp", "mrow", "mcol"))
    row_full = lax.dynamic_slice(summed, (row_base,), (shard_rows,))
    col_full = lax.dynamic_slice(summed, (width_all + col_base,), (shard_cols,))
    grand_total = jnp.sum(summed[:width_all])
    row_mine = lax.dynamic_slice(row_old, (row_base,), (shard_rows,))
    col_mine = lax.dynamic_slice(col_old, (col_base,), (shard_cols,))
    row_factor = SECOND_DECAY * row_mine + (1.0 - SECOND_DECAY) * (
        row_full / outputs_all + SQUARE_EPS
    )
    col_factor = SECOND_DECAY * col_mine + (1.0 - SECOND_DECAY) * (
        col_full / width_all + SQUARE_EPS
    )
    row_mean = (
        SECOND_DECAY * jnp.sum(row_old)
        + (1.0 - SECOND_DECAY) * (grand_total / outputs_all + width_all * SQUARE_EPS)
    ) / width_all
    direction = grad / jnp.sqrt(row_factor[:, None] * col_factor[None, :] / row_mean)
    entries = width_all * outputs_all
    update_sq, weight_sq = lax.psum(
        (jnp.sum(direction * direction), jnp.sum(weight * weight)), ("dp", "mrow", "mcol")
    )
    clip_factor = jnp.maximum(1.0, jnp.sqrt(update_sq / entries))
    weight_scale = jnp.sqrt(weight_sq / entries)
    scaled_step = weight_scale * direction / clip_factor
    new_weight = weight - STEP_RATE * scaled_step
    weight_half = new_weight.astype(jnp.bfloat16)
    inputs = next_input
    block_sum = jnp.dot(
        inputs,
        lax.all_gather(weight_half, "dp", axis=0, tiled=True),
        preferred_element_type=jnp.float32,
    )
    summed_out = lax.psum_scatter(block_sum, "mrow", scatter_dimension=0, tiled=True)
    queries = summed_out * width_all ** (-0.5)
    return (new_weight, row_factor, col_factor, queries, scaled_step)


def solution(mesh):
    placed = (
        P(("mrow", "dp"), "mcol"),
        P("dp", "mrow"),
        P("dp", "mcol"),
        P(),
        P(),
        P("dp", "mrow"),
    )
    return jax.shard_map(
        body,
        mesh=mesh,
        in_specs=placed,
        out_specs=(
            P(("mrow", "dp"), "mcol"),
            P(("mrow", "dp")),
            P("mcol"),
            P(("dp", "mrow"), "mcol"),
            P(("mrow", "dp"), "mcol"),
        ),
        check_vma=False,
    )
```

profile of v0, /device:TPU:8, one launch (start us, length us, event | category | flops | bytes accessed | tf_op | source)
XLA Modules:
  0.0 850.5 jit_solution(12053091211510706755)
XLA Ops:
  7.2 0.0 reduce-scatter.3.cloned.1.call-start
  7.2 1.2 copy-done
  8.4 12.5 %fusion.1 = f32[2304,3072]{1,0:T(8,128)} fusion(bf16[192,2304]{1,0:T(8,128)(2,1)} %param.7, bf16[192,3072]{1,0:T(8,128)(2,1)S(1)} %copy-done), kind=kOutput, calls=%fused_computation.13 | convolution fusion | flops 2717908992 | bytes 30375936 | tf_op jit(solution)/shard_map/dot_general | solution.py:20
  21.0 0.0 all-reduce.3.cloned.1.call-start
  21.0 285.0 %reduce-scatter.3.cloned.1.call-done = f32[288,3072]{1,0:T(8,128)} async-done(((f32[2304,3072]{1,0:T(8,128)}), f32[288,3072]{1,0:T(8,128)}) %reduce-scatter.3.cloned.1.call-update) | async-done | bytes 3538960 | tf_op jit(solution)/shard_map/reduce_scatter | solution.py:19
  306.1 2.5 multiply_reduce_fusion.2
  308.5 0.3 dynamic_update_slice.6
  308.8 0.3 dynamic_update_slice.7
  309.2 0.6 copy-done.1
  309.8 0.0 all-gather.2.cloned.1.call-start
  309.9 3.5 multiply_reduce_fusion.1
  313.4 0.6 reduce_sum.57
  314.7 238.2 %all-reduce.3.cloned.1.call-done = f32[30720]{0:T(1024)} async-done(((f32[30720]{0:T(1024)}), f32[30720]{0:T(1024)}) %all-reduce.3.cloned.1.call-update) | async-done | bytes 122896 | tf_op jit(solution)/shard_map/psum | solution.py:33
  552.8 1.5 slice_reduce_fusion
  555.0 0.8 multiply_add_fusion.1
  555.8 0.7 multiply_add_fusion
  556.5 3.6 multiply_reduce_fusion
  560.1 73.1 %all-reduce = (f32[]{:T(128)}, f32[]{:T(128)}) all-reduce(f32[]{:T(128)} %multiply_reduce_fusion, f32[]{:T(128)} %multiply_reduce_fusion.1), channel_id=1, replica_groups=mesh['dp'=8,'mrow'=8,'mcol'=4] {'dp','mrow','mcol'}, use_global_device_ids=true, to_apply=%region_9.0 | all-reduce | flops 2 | bytes 16 | tf_op jit(solution)/shard_map/psum | solution.py:51
  634.7 8.4 fusion
  643.1 0.0 reduce-scatter.5.cloned.1.call-start
  643.1 145.7 %all-gather.2.cloned.1.call-done = bf16[2304,3072]{1,0:T(8,128)(2,1)} async-done(((bf16[288,3072]{1,0:T(8,128)(2,1)}), bf16[2304,3072]{1,0:T(8,128)(2,1)}) %all-gather.2.cloned.1.call-update) | async-done | bytes 14155792 | tf_op jit(solution)/shard_map/all_gather | solution.py:62
  788.8 9.4 %convolution_bitcast_fusion = f32[192,3072]{1,0:T(8,128)} fusion(bf16[192,2304]{1,0:T(8,128)(2,1)S(1)} %copy-done.5, bf16[2304,3072]{1,0:T(8,128)(2,1)} %all-gather.2.cloned.1.call-done), kind=kOutput, calls=%fused_computation | convolution fusion | flops 2717908992 | bytes 17399808 | tf_op jit(solution)/shard_map/dot_general | solution.py:60
  798.3 43.9 %reduce-scatter.5.cloned.1.call-done = f32[24,3072]{1,0:T(8,128)} async-done(((f32[192,3072]{1,0:T(8,128)}), f32[24,3072]{1,0:T(8,128)}) %reduce-scatter.5.cloned.1.call-update) | async-done | bytes 294928 | tf_op jit(solution)/shard_map/reduce_scatter | solution.py:65
  842.2 1.7 broadcast_multiply_fusion
  (15 shorter events, 0.1 us)
Async XLA Ops:
  7.2 1.3 copy-start
  7.2 298.9 %reduce-scatter.3.cloned.1.call-start = ((), (), s32[]{:S(2)}) async-start(), calls=%async_computation.2 | async-start | bytes 31850496 | tf_op jit(solution)/shard_map/reduce_scatter | solution.py:19
  21.0 531.9 %all-reduce.3.cloned.1.call-start = ((), (), s32[]{:S(2)}) async-start(), calls=%async_computation.3 | async-start | bytes 245760 | tf_op jit(solution)/shard_map/psum | solution.py:33
  21.0 292.4 %copy-start.3 = (f32[18432]{0:T(1024)S(1)}, f32[18432]{0:T(1024)}, u32[]{:S(2)}) copy-start(f32[18432]{0:T(1024)} %param.9) | copy-start | bytes 221188
  309.1 0.7 copy-start.1
  309.8 479.0 %all-gather.2.cloned.1.call-start = ((), (), s32[]{:S(2)}) async-start(), calls=%async_computation.4 | async-start | bytes 15925248 | tf_op jit(solution)/shard_map/all_gather | solution.py:62
  555.8 87.3 %copy-start.4 = (f32[288]{0:T(512)}, f32[288]{0:T(512)S(1)}, u32[]{:S(2)}) copy-start(f32[288]{0:T(512)S(1)} %multiply_add_fusion.1) | copy-start | bytes 3460
  556.5 86.5 %copy-start.2 = (f32[3072]{0:T(1024)}, f32[3072]{0:T(1024)S(1)}, u32[]{:S(2)}) copy-start(f32[3072]{0:T(1024)S(1)} %multiply_add_fusion) | copy-start | bytes 36868
  634.6 154.2 %copy-start.5 = (bf16[192,2304]{1,0:T(8,128)(2,1)S(1)}, bf16[192,2304]{1,0:T(8,128)(2,1)}, u32[]{:S(2)}) copy-start(bf16[192,2304]{1,0:T(8,128)(2,1)} %param.11) | copy-start | bytes 2654212
  643.1 199.2 %reduce-scatter.5.cloned.1.call-start = ((), (), s32[]{:S(2)}) async-start(), calls=%async_computation.5 | async-start | bytes 2654208 | tf_op jit(solution)/shard_map/reduce_scatter | solution.py:65
Sparse Core Ops, SparseCore 0:
  21.1 284.9 reduce-scatter.2
  312.1 240.6 all-reduce.2
  643.2 145.5 all-gather.1
  798.4 43.7 reduce-scatter.4
where the time goes:
time: 852 us; the launch traced here: 850 us
  waiting for transfers between devices  713 us (84%)
  blocking collectives  73.1 us (9%)
  other arithmetic  23.3 us (3%)
  matrix products  21.9 us (3%)
  between operations  16.5 us (2%)
    reduce_scatter x1, waiting for transfers between devices, body(): lax.psum_scatter(lax.dot_general(inputs, cotangent, (((0,), (0,)), ((), (...  285 us
    psum x1, waiting for transfers between devices, body(): summed = lax.psum(vector, ('dp', 'mrow', 'mcol'))  238 us
    all_gather x1, waiting for transfers between devices, body(): lax.all_gather(weight_half, 'dp', axis=0, tiled=True)  146 us
    psum x1, blocking collectives, body(): lax.psum((jnp.sum(direction * direction), jnp.sum(weight * weight)), ('dp...  73.1 us
    reduce_scatter x1, waiting for transfers between devices, body(): lax.psum_scatter(block_sum, 'mrow', scatter_dimension=0, tiled=True)  43.9 us
  transfers between devices with their start and end apart: 4, of which 4 were waited for; matrix products, arithmetic and copies ran while one was open for 0% of the time, Pallas kernels for 0%

commit v1 on v0

v1 whole, which is shorter than its diff:
```python
import jax
import jax.numpy as jnp
from jax import lax
from jax.experimental import pallas as pl
from jax.experimental.pallas import tpu as pltpu
from jax.sharding import PartitionSpec as P

SECOND_DECAY = 1.0 - 10.0 ** (-0.8)
SQUARE_EPS = 1e-30
STEP_RATE = 0.01

NZ = 8
NX = 4
TOK = 192
D = 18432
QW = 12288
TOKENS = 1536
FEAT = 288
BLOCK = 2304
COLS = 3072
HALF = 96
QTOK = 24
Z_COLS = 1024
X_BASE = 1024
X_COLS = 512
SLICE = COLS // NZ
CHUNK = 512
NCHUNK = COLS // CHUNK
SLOTS = 3
N_SEM = 256
MESH = pl.DeviceIdType.MESH
HI = lax.Precision.HIGHEST
F32 = jnp.float32
BF16 = jnp.bfloat16


def rot(base, step, size):
    return lax.rem(base + (step + size) % size, size)


def aligned(start, size, mult):
    return pl.ds(pl.multiple_of(start, mult), size)


def kernel(
    cot_hbm, act_hbm, nxt_hbm, w_hbm, row_old, row_mine, col_mine,
    g_out, q_out, rf_out, cf_out, sc_out,
    cot, grad, w_buf, act, act_s, act_all, act_t, nxt, nxt_s, nxt_y, nxt_all,
    row_acc, row_send, row_recv, vec, vec_z, vec_xy, scal, col_row,
    w_own, w_peer, part, opp_send, opp_recv, x_send, x_recv, z_send, z_recv,
    local_sem, send_sem, recv_sem,
):
    dp = lax.axis_index("dp")
    mr = lax.axis_index("mrow")
    mc = lax.axis_index("mcol")
    x = lax.rem(mr, NX)
    y = lax.div(mr, NX)
    core = lax.rem(mc, 2)
    sib = mc + 1 - 2 * core
    ymate = (1 - y) * NX + x
    count = [0]
    sent = []

    def remote(src, dst, dev):
        i = count[0]
        count[0] += 1
        return pltpu.make_async_remote_copy(
            src_ref=src, dst_ref=dst, send_sem=send_sem.at[i], recv_sem=recv_sem.at[i],
            device_id=dev, device_id_type=MESH,
        )

    def go(copy):
        copy.start()
        sent.append(copy)
        return copy

    def zdev(k):
        return {"dp": rot(dp, k, NZ)}

    def xdev(k):
        return {"mrow": y * NX + rot(x, k, NX)}

    def zrows(k):
        return aligned(rot(dp, k, NZ) * TOK, TOK, 64)

    own = zrows(0)
    loads = [
        pltpu.make_async_copy(cot_hbm, cot.at[own], local_sem.at[0]),
        pltpu.make_async_copy(act_hbm, act, local_sem.at[1]),
        pltpu.make_async_copy(nxt_hbm, nxt, local_sem.at[2]),
        pltpu.make_async_copy(w_hbm, w_buf, local_sem.at[3]),
    ]
    for load in loads:
        load.start()

    barrier = pltpu.get_barrier_semaphore()
    for k in range(1, NZ):
        pl.semaphore_signal(barrier, inc=1, device_id=zdev(k), device_id_type=MESH)
        pl.semaphore_signal(
            barrier, inc=1, device_id={"mrow": rot(mr, k, NZ)}, device_id_type=MESH
        )
    for k in range(1, 4):
        pl.semaphore_signal(
            barrier, inc=1, device_id={"mcol": rot(mc, k, 4)}, device_id_type=MESH
        )
    loads[0].wait()
    pl.semaphore_wait(barrier, 17)

    x_start = X_BASE + x * X_COLS
    flows = [
        (pl.multiple_of(x_start, 128), X_COLS, True),
        (0, Z_COLS // 2, False),
        (Z_COLS // 2, Z_COLS // 2, False),
    ]

    def z_send_step(flow, sign, s):
        start, width, _ = flow
        if s == 4:
            width = width // 2
            if sign < 0:
                start = start + width
        if not isinstance(start, int):
            start = pl.multiple_of(start, 128)
        ref = cot.at[zrows(-sign * (s - 1)), pl.ds(start, width)]
        return go(remote(ref, ref, zdev(sign)))

    step = {}
    for f, flow in enumerate(flows):
        for sign in (1, -1):
            step[f, sign, 1] = z_send_step(flow, sign, 1)

    loads[1].wait()
    for k in range(NZ):
        act_s[k] = act[:, k * FEAT:(k + 1) * FEAT]
    core_rows = pl.multiple_of(core * HALF, 32)
    act_in = {}
    for k in range(1, NZ):
        act_in[k] = go(remote(
            act_s.at[rot(dp, k, NZ), pl.ds(core_rows, HALF)],
            act_all.at[aligned(dp * TOK + core * HALF, HALF, 32)],
            zdev(k),
        ))
    act_all[own] = act_s[dp]

    loads[2].wait()
    for k in range(NZ):
        nxt_s[k] = nxt[:, k * FEAT:(k + 1) * FEAT]

    loads[3].wait()

    def weight_square(i, total):
        tile = w_buf[:, aligned(i * 256, 256, 256)]
        return total + jnp.sum((tile * tile).reshape(FEAT // 8, 8, 256), axis=0)

    wsq = lax.fori_loop(0, COLS // 256, weight_square, jnp.zeros((8, 256), F32))
    vec[...] = jnp.zeros((8, COLS), F32) + jnp.sum(wsq)

    def x_quarter(k, q, part_of, dev):
        width = X_COLS
        start = X_BASE + q * X_COLS
        if part_of is not None:
            width = X_COLS // 2
            start = start + part_of * width
        ref = cot.at[zrows(k), pl.ds(pl.multiple_of(start, 128), width)]
        return go(remote(ref, ref, dev))

    direct = {}
    forward = {}

    def x_piece(k):
        for sign in (1, -1):
            direct[k, sign] = x_quarter(k, x, None, xdev(sign))

    def x_forward(k):
        for sign in (1, -1):
            direct[k, sign].wait_recv()
            forward[k, sign] = x_quarter(k, rot(x, -sign, NX), 0 if sign > 0 else 1, xdev(sign))

    act_fwd = {}

    def act_forward(k):
        act_in[k].wait_recv()
        ref = act_all.at[aligned(rot(dp, -k, NZ) * TOK + core * HALF, HALF, 32)]
        act_fwd[k] = go(remote(ref, ref, {"mcol": sib}))

    for s in range(1, 5):
        for f, flow in enumerate(flows):
            for sign in (1, -1):
                step[f, sign, s].wait_recv()
                if s < 4:
                    step[f, sign, s + 1] = z_send_step(flow, sign, s + 1)
            if flow[2]:
                if s < 4:
                    x_piece(-s)
                    x_piece(s)
                else:
                    x_piece(4)
        if s > 1:
            x_forward(-(s - 1))
            x_forward(s - 1)
        if s == 2:
            for k in (1, 7, 2, 6):
                act_forward(k)
        if s == 3:
            for k in (3, 5, 4):
                act_forward(k)

    y_rows = pl.multiple_of(y * HALF, 32)
    o_rows = pl.multiple_of((1 - y) * HALF, 32)
    nxt_mate = go(remote(nxt_s.at[:, pl.ds(o_rows, HALF)], nxt_y, {"mrow": ymate}))
    nxt_in = {}
    for k in range(1, NZ):
        nxt_in[0, k] = go(remote(
            nxt_s.at[rot(dp, k, NZ), pl.ds(y_rows, HALF)],
            nxt_all.at[0, aligned(dp * HALF, HALF, 32)],
            zdev(k),
        ))
    nxt_all[0, aligned(dp * HALF, HALF, 32), :] = nxt_s[dp, pl.ds(y_rows, HALF), :]

    for k in range(1, NZ):
        act_fwd[k].wait_recv()
    for i in range(4):
        rows = slice(i * 384, (i + 1) * 384)
        act_t[:, rows] = act_all[rows, :].T
    row_acc[...] = jnp.zeros((FEAT, 128), F32)

    def grad_tiles(base, tiles):
        def one(i, carry):
            cols = aligned(base + i * 256, 256, 256)
            g = jnp.dot(act_t[...], cot[:, cols], preferred_element_type=F32)
            grad[:, cols] = g
            sq = g * g
            row_acc[...] += sq[:, :128] + sq[:, 128:]
            vec[0:1, cols] = jnp.sum(sq, axis=0, keepdims=True)
            return carry

        lax.fori_loop(0, tiles, one, 0)

    grad_tiles(0, Z_COLS // 256)
    grad_tiles(X_BASE + x * X_COLS, X_COLS // 256)
    x_forward(4)
    grad_tiles(X_BASE + rot(x, 1, NX) * X_COLS, X_COLS // 256)
    grad_tiles(X_BASE + rot(x, 3, NX) * X_COLS, X_COLS // 256)
    for k in (-1, 1, -2, 2, -3, 3, 4):
        for sign in (1, -1):
            forward[k, sign].wait_recv()
    grad_tiles(X_BASE + rot(x, 2, NX) * X_COLS, X_COLS // 256)
    g_copy = pltpu.make_async_copy(grad, g_out, local_sem.at[4])
    g_copy.start()

    ones = jnp.ones((8, 128), F32)
    row_send[...] = lax.dot_general(
        ones, row_acc[...], (((1,), (1,)), ((), ())), precision=HI, preferred_element_type=F32
    )
    row_in = [
        go(remote(row_send, row_recv.at[k], {"mcol": rot(mc, k, 4)})) for k in range(1, 4)
    ]
    nxt_mate.wait_recv()
    for k in range(1, NZ):
        nxt_in[1, k] = go(remote(
            nxt_y.at[rot(dp, k, NZ)],
            nxt_all.at[1, aligned(dp * HALF, HALF, 32)],
            zdev(k),
        ))
    nxt_all[1, aligned(dp * HALF, HALF, 32), :] = nxt_y[dp]
    for copy in row_in:
        copy.wait_recv()
    row_full = ((row_send[...] + row_recv[1]) + row_recv[2]) + row_recv[3]
    row_factor = SECOND_DECAY * row_mine[...] + (1.0 - SECOND_DECAY) * (
        row_full * (1.0 / QW) + SQUARE_EPS
    )
    rf_out[...] = row_factor[0:1]
    row_inv = lax.dot_general(
        1.0 / row_factor, ones * 0.125, (((0,), (0,)), ((), ())), precision=HI,
        preferred_element_type=F32,
    )
    row_root = jnp.sqrt(row_inv)

    def weighted(i, carry):
        cols = aligned(i * 256, 256, 256)
        g = grad[:, cols]
        vec[1:2, cols] = jnp.sum(g * g * row_inv[:, 0:1], axis=0, keepdims=True)
        return carry

    lax.fori_loop(0, COLS // 256, weighted, 0)

    def vslice(k):
        return aligned(rot(dp, k, NZ) * SLICE, SLICE, 128)

    z_in = [
        go(remote(vec.at[:, vslice(k)], vec_z.at[k], zdev(k))) for k in range(1, NZ)
    ]
    total = vec[:, vslice(0)]
    for k in range(1, NZ):
        z_in[k - 1].wait_recv()
        total = total + vec_z[k]
    vec_xy[0] = total
    xy_in = [
        go(remote(vec_xy.at[0], vec_xy.at[k], {"mrow": rot(mr, k, NZ)}))
        for k in range(1, NZ)
    ]
    for k in range(1, NZ):
        xy_in[k - 1].wait_recv()
        total = total + vec_xy[k]
    vec_z[0] = total
    full_in = []
    for k in range(1, NZ):
        full_in.append(go(remote(vec_z.at[0], scal.at[0, :, vslice(0)], zdev(k))))
    scal[0, :, vslice(0)] = total
    for copy in full_in:
        copy.wait_recv()
    col_factor = SECOND_DECAY * col_mine[...] + (1.0 - SECOND_DECAY) * (
        scal[0, 0:1, :] * (1.0 / D) + SQUARE_EPS
    )
    cf_out[...] = col_factor
    square_total = jnp.sum(scal[0, 0:1, :])
    update_total = jnp.sum(scal[0, 1:2, :] / col_factor)
    w_total = scal[0, 2:3, 0:128]
    scal[1, 0:1, 0:128] = jnp.zeros((1, 128), F32) + square_total
    scal[1, 1:2, 0:128] = jnp.zeros((1, 128), F32) + update_total
    scal[1, 2:3, 0:128] = w_total
    scal[1, 3:8, 0:128] = jnp.zeros((5, 128), F32)
    s_in = [
        go(remote(
            scal.at[1, :, pl.ds(0, 128)], scal.at[1, :, pl.ds(k * 128, 128)],
            {"mcol": rot(mc, k, 4)},
        ))
        for k in range(1, 4)
    ]
    old_total = jnp.sum(row_old[...])
    for copy in s_in:
        copy.wait_recv()
    sums = (
        (scal[1, :, 0:128] + scal[1, :, 128:256]) + scal[1, :, 256:384]
    ) + scal[1, :, 384:512]
    row_mean = (
        SECOND_DECAY * old_total
        + (1.0 - SECOND_DECAY) * (sums[0:1] * (1.0 / QW) + D * SQUARE_EPS)
    ) * (1.0 / D)
    entries = float(D) * float(QW)
    clip = jnp.maximum(1.0, jnp.sqrt(row_mean * sums[1:2] * (1.0 / entries)))
    w_scale = jnp.sqrt(sums[2:3] * (1.0 / entries))
    scale = w_scale * jnp.sqrt(row_mean) / clip
    sc_out[...] = jnp.zeros((8, 128), F32) + scale
    col_scale = (STEP_RATE * scale[0:1, 0:1]) * lax.rsqrt(col_factor)

    col_row[...] = col_scale
    w_in = []
    for c in range(NCHUNK):
        def update(i, carry, c=c):
            cols = aligned(c * CHUNK + i * 256, 256, 256)
            new_w = w_buf[:, cols] - grad[:, cols] * (row_root[:, 0:1] * col_row[0:1, cols])
            w_own[:, cols] = new_w.astype(BF16)
            return carry

        lax.fori_loop(0, CHUNK // 256, update, 0)
        cols = pl.ds(c * CHUNK, CHUNK)
        w_in.append(go(remote(w_own.at[:, cols], w_peer.at[:, cols], {"mrow": ymate})))
    for copy in nxt_in.values():
        copy.wait_recv()

    opp_in = {}
    x_in = {}
    z_part = {}
    x_next = rot(x, 1, NX)
    x_prev = rot(x, 3, NX)
    x_opp = rot(x, 2, NX)
    hw = CHUNK // 2

    def block(c, q, cols=slice(None)):
        return part[c % SLOTS, :, q, :, cols].reshape(NZ * QTOK, -1)

    def stage_matmul(c):
        w_in[c].wait_recv()

        def one(i, carry):
            src = aligned(c * CHUNK + i * 256, 256, 256)
            for r in range(2):
                rows = slice(r * 384, (r + 1) * 384)
                p = jnp.dot(nxt_all[0, rows, :], w_own[:, src], preferred_element_type=F32)
                p = p + jnp.dot(nxt_all[1, rows, :], w_peer[:, src], preferred_element_type=F32)
                part[c % SLOTS, r * 4:(r + 1) * 4, :, :, aligned(i * 256, 256, 256)] = (
                    p.reshape(4, NX, QTOK, 256)
                )
            return carry

        lax.fori_loop(0, CHUNK // 256, one, 0)
        opp_send[c, 0] = block(c, x_opp, slice(0, hw)).astype(BF16)
        opp_send[c, 1] = block(c, x_opp, slice(hw, CHUNK)).astype(BF16)
        for j, sign in ((0, 1), (1, -1)):
            opp_in[c, j] = go(remote(opp_send.at[c, j], opp_recv.at[c, j], xdev(sign)))

    def stage_relay(c):
        opp_in[c, 0].wait_recv()
        x_send[c, 0, :, 0:hw] = (
            block(c, x_next, slice(0, hw)) + opp_recv[c, 0].astype(F32)
        ).astype(BF16)
        x_send[c, 0, :, hw:CHUNK] = block(c, x_next, slice(hw, CHUNK)).astype(BF16)
        x_in[c, 0] = go(remote(x_send.at[c, 0], x_recv.at[c, 0], xdev(1)))
        opp_in[c, 1].wait_recv()
        x_send[c, 1, :, hw:CHUNK] = (
            block(c, x_prev, slice(hw, CHUNK)) + opp_recv[c, 1].astype(F32)
        ).astype(BF16)
        x_send[c, 1, :, 0:hw] = block(c, x_prev, slice(0, hw)).astype(BF16)
        x_in[c, 1] = go(remote(x_send.at[c, 1], x_recv.at[c, 1], xdev(-1)))

    def stage_z(c):
        x_in[c, 0].wait_recv()
        x_in[c, 1].wait_recv()
        summed = (
            block(c, x) + x_recv[c, 0].astype(F32) + x_recv[c, 1].astype(F32)
        ).reshape(NZ, QTOK, CHUNK)
        part[c % SLOTS, :, x, :, :] = summed
        z_send[c] = jnp.concatenate(
            [summed[:, :, :hw], summed[:, :, hw:]], axis=1
        ).astype(BF16)
        for k in range(1, NZ):
            z_part[c, k] = go(remote(
                z_send.at[c, rot(dp, k, NZ)], z_recv.at[c, k], zdev(k)
            ))
        q_out[:, c * CHUNK:(c + 1) * CHUNK] = part[c % SLOTS, dp, x, :, :]

    def stage_out(c):
        acc = None
        for k in range(1, NZ):
            z_part[c, k].wait_recv()
            term = z_recv[c, k].astype(F32)
            acc = term if acc is None else acc + term
        for j in range(2):
            cols = slice(c * CHUNK + j * hw, c * CHUNK + (j + 1) * hw)
            q_out[:, cols] = (q_out[:, cols] + acc[j * QTOK:(j + 1) * QTOK]) * D ** (-0.5)

    for t in range(NCHUNK + 3):
        if t < NCHUNK:
            stage_matmul(t)
        if 0 <= t - 1 < NCHUNK:
            stage_relay(t - 1)
        if 0 <= t - 2 < NCHUNK:
            stage_z(t - 2)
        if 0 <= t - 3 < NCHUNK:
            stage_out(t - 3)

    g_copy.wait()
    for copy in sent:
        copy.wait_send()


def body(weight, activations, cotangent, row_old, col_old, next_input):
    row_base = (lax.axis_index("mrow") * NZ + lax.axis_index("dp")) * FEAT
    col_base = lax.axis_index("mcol") * COLS
    row_mine = lax.dynamic_slice(row_old, (row_base,), (FEAT,)).reshape(1, FEAT)
    col_mine = lax.dynamic_slice(col_old, (col_base,), (COLS,)).reshape(1, COLS)
    vm = pl.BlockSpec(memory_space=pltpu.VMEM)
    hbm = pl.BlockSpec(memory_space=pl.ANY)
    v = pltpu.VMEM
    grad, queries, row_factor, col_factor, scale = pl.pallas_call(
        kernel,
        out_shape=(
            jax.ShapeDtypeStruct((FEAT, COLS), F32),
            jax.ShapeDtypeStruct((QTOK, COLS), F32),
            jax.ShapeDtypeStruct((1, FEAT), F32),
            jax.ShapeDtypeStruct((1, COLS), F32),
            jax.ShapeDtypeStruct((8, 128), F32),
        ),
        in_specs=[hbm, hbm, hbm, hbm, vm, vm, vm],
        out_specs=(hbm, vm, vm, vm, vm),
        scratch_shapes=[
            v((TOKENS, COLS), BF16),
            v((FEAT, COLS), F32),
            v((FEAT, COLS), F32),
            v((TOK, BLOCK), BF16),
            v((NZ, TOK, FEAT), BF16),
            v((TOKENS, FEAT), BF16),
            v((FEAT, TOKENS), BF16),
            v((TOK, BLOCK), BF16),
            v((NZ, TOK, FEAT), BF16),
            v((NZ, HALF, FEAT), BF16),
            v((2, TOKENS // 2, FEAT), BF16),
            v((FEAT, 128), F32),
            v((8, FEAT), F32),
            v((4, 8, FEAT), F32),
            v((8, COLS), F32),
            v((NZ, 8, SLICE), F32),
            v((NZ, 8, SLICE), F32),
            v((2, 8, COLS), F32),
            v((1, COLS), F32),
            v((FEAT, COLS), BF16),
            v((FEAT, COLS), BF16),
            v((SLOTS, NZ, NX, QTOK, CHUNK), F32),
            v((NCHUNK, 2, TOK, CHUNK // 2), BF16),
            v((NCHUNK, 2, TOK, CHUNK // 2), BF16),
            v((NCHUNK, 2, TOK, CHUNK), BF16),
            v((NCHUNK, 2, TOK, CHUNK), BF16),
            v((NCHUNK, NZ, 2 * QTOK, CHUNK // 2), BF16),
            v((NCHUNK, NZ, 2 * QTOK, CHUNK // 2), BF16),
            pltpu.SemaphoreType.DMA((5,)),
            pltpu.SemaphoreType.DMA((N_SEM,)),
            pltpu.SemaphoreType.DMA((N_SEM,)),
        ],
        compiler_params=pltpu.CompilerParams(
            collective_id=0, has_side_effects=True, vmem_limit_bytes=60 * 1024 * 1024
        ),
        cost_estimate=pl.CostEstimate(
            flops=4 * TOKENS * FEAT * COLS, bytes_accessed=16_000_000, transcendentals=0
        ),
        name="update",
    )(
        cotangent, activations, next_input, weight,
        row_old.reshape(D // 128, 128), row_mine, col_mine,
    )
    row_factor = row_factor.reshape(FEAT)
    col_factor = col_factor.reshape(COLS)
    factor = scale[0, 0] * lax.rsqrt(row_factor)
    scaled_step = grad * (factor[:, None] * lax.rsqrt(col_factor)[None, :])
    new_weight = weight - STEP_RATE * scaled_step
    return (new_weight, row_factor, col_factor, queries, scaled_step)


def solution(mesh):
    placed = (
        P(("mrow", "dp"), "mcol"),
        P("dp", "mrow"),
        P("dp", "mcol"),
        P(),
        P(),
        P("dp", "mrow"),
    )
    return jax.shard_map(
        body,
        mesh=mesh,
        in_specs=placed,
        out_specs=(
            P(("mrow", "dp"), "mcol"),
            P(("mrow", "dp")),
            P("mcol"),
            P(("dp", "mrow"), "mcol"),
            P(("mrow", "dp"), "mcol"),
        ),
        check_vma=False,
    )
```

time: 852 us -> 195 us (0.23)
  waiting for transfers between devices: 713 us -> 0 us
  Pallas kernels: 0 us -> 181 us
  blocking collectives: 73.1 us -> 0 us
  matrix products: 21.9 us -> 0 us
  other arithmetic: 23.3 us -> 7.48 us
  between operations: 16.5 us -> 0.69 us
    reduce_scatter x2 -> x0, waiting for transfers between devices: 329 us -> none  [the longest x1 285 us: body(): lax.psum_scatter(lax.dot_general(inputs, cotangent, (((0,), (0,)), ((), (...]
    psum x1 -> x0, waiting for transfers between devices: 238 us -> none  [body(): summed = lax.psum(vector, ('dp', 'mrow', 'mcol'))]
    pallas_call x0 -> x1, Pallas kernels: none -> 181 us  [body(): pl.pallas_call(kernel, out_shape=(jax.ShapeDtypeStruct((FEAT, COLS), F32)...]
    all_gather x1 -> x0, waiting for transfers between devices: 146 us -> none  [body(): lax.all_gather(weight_half, 'dp', axis=0, tiled=True)]
    psum x1 -> x0, blocking collectives: 73.1 us -> none  [body(): lax.psum((jnp.sum(direction * direction), jnp.sum(weight * weight)), ('dp...]
    dot_general x2 -> x0, matrix products: 22 us -> none  [the longest x1 12.5 us: body(): lax.dot_general(inputs, cotangent, (((0,), (0,)), ((), ())), preferred_el...]
    reduce_sum x5 -> x0, other arithmetic: 11.7 us -> none  [the longest x1 3.6 us: body(): jnp.sum(direction * direction)]
  transfers between devices with their start and end apart: 4 -> 0, of which waited for: 4 -> 0; matrix products, arithmetic and copies ran while one was open for 0% -> 0% of each run, Pallas kernels for 0% -> 0%
where the time goes in v1:
time: 195 us
  Pallas kernels  181 us (93%)
  other arithmetic  7.48 us (4%)
  local copies, waits for them, and re-layouts  5.9 us (3%)
    pallas_call x1, Pallas kernels, body(): pl.pallas_call(kernel, out_shape=(jax.ShapeDtypeStruct((FEAT, COLS), F32)...  181 us
    sub x1, other arithmetic, body(): new_weight = weight - STEP_RATE * scaled_step  6.16 us

profile of v1, /device:TPU:8, one launch (start us, length us, event | category | flops | bytes accessed | tf_op | source)
XLA Modules:
  0.0 194.9 jit_solution(13046101246813429097)
XLA Ops:
  0.6 0.8 dynamic_slice.6
  1.4 0.6 reshape.32.row_mine
  2.0 1.3 dynamic_slice.7
  3.3 0.0 copy-start
  3.3 180.8 %update.1 = (f32[288,3072]{1,0:T(8,128)}, f32[24,3072]{1,0:T(8,128)}, f32[1,288]{1,0:T(1,128)}, f32[1,3072]{1,0:T(1,128)}, f32[8,128]{1,0:T(8,128)}) custom-call(bf16[192,3072]{1,0:T(8,128)(2,1)} %cot_hbm.1, bf16[192,2304]{1,0:T(8,128)(2,1)} %act_hbm.1, bf16[192,2304]{1,0:T(8,128)(2,1)} %nxt_hbm.1, f32[288,3072]{1,0:T(8,128)} %w_hbm.1, f32[144,128]{1,0:T(8,128)} %bitcast.8, ...), custom_call_target="tpu_custom_call" | custom-call | flops 5435817984 | bytes 16000000 | tf_op jit(solution)/shard_map/update/pallas_call | solution.py:456
  184.1 1.2 slice.3
  185.3 0.7 reduce
  186.0 0.0 copy-start.3
  186.0 0.7 rsqrt_multiply_fusion
  186.7 0.7 rsqrt.12
  187.4 0.0 copy-done
  187.4 0.0 copy-start.2
  187.4 0.0 copy-start.1
  187.4 6.2 %multiply_subtract_fusion = (f32[288,3072]{1,0:T(8,128)}, f32[288,3072]{1,0:T(8,128)}) fusion(f32[288,3072]{1,0:T(8,128)S(1)} %copy-done, f32[288,3072]{1,0:T(8,128)} %get-tuple-element.10, f32[3072]{0:T(1024)S(1)} %bitcast.5, f32[288]{0:T(512)S(1)} %rsqrt_multiply_fusion), kind=kLoop, calls=%fused_computation | loop fusion | flops 3538944 | bytes 14169216 | tf_op jit(solution)/shard_map/sub | solution.py:515
  193.6 0.0 copy-done.3
  193.6 0.0 copy-done.2
  193.6 0.6 copy.13
  194.2 0.0 copy-done.1
  194.2 0.7 copy.14
Async XLA Ops:
  3.3 184.1 %copy-start = (f32[288,3072]{1,0:T(8,128)S(1)}, f32[288,3072]{1,0:T(8,128)}, u32[]{:S(2)}) copy-start(f32[288,3072]{1,0:T(8,128)} %w_hbm.1) | copy-start | bytes 10616836
  186.0 7.6 %copy-start.3 = (f32[288]{0:T(512)}, f32[288]{0:T(512)S(1)}, u32[]{:S(2)}) copy-start(f32[288]{0:T(512)S(1)} %reduce) | copy-start | bytes 3460
  187.4 6.2 %copy-start.2 = (f32[1,3072]{1,0:T(1,128)S(1)}, f32[1,3072]{1,0:T(1,128)}, u32[]{:S(2)}) copy-start(f32[1,3072]{1,0:T(1,128)} %get-tuple-element.13) | copy-start | bytes 36868
  187.4 6.8 %copy-start.1 = (f32[24,3072]{1,0:T(8,128)S(1)}, f32[24,3072]{1,0:T(8,128)}, u32[]{:S(2)}) copy-start(f32[24,3072]{1,0:T(8,128)} %get-tuple-element.25) | copy-start | bytes 884740

commit v2 on v0

v2 whole, which is shorter than its diff:
```python
import jax
import jax.numpy as jnp
from jax import lax
from jax.experimental import pallas as pl
from jax.experimental.pallas import tpu as pltpu
from jax.sharding import PartitionSpec as P

SECOND_DECAY = 1.0 - 10.0 ** (-0.8)
SQUARE_EPS = 1e-30
STEP_RATE = 0.01

NZ = 8
NX = 4
PLANE = 32
TOK = 192
D = 18432
QW = 12288
TOKENS = 1536
FEAT = 288
BLOCK = 2304
COLS = 3072
HALF = 96
QTOK = 24
B_COLS = 128
E_BASE = 512
E_COLS = 768
H_BASE = 2048
H_COLS = 256
WIDTHS = (256, 256, 512, 512, 512, 512, 256, 256)
STARTS = tuple(sum(WIDTHS[:i]) for i in range(len(WIDTHS)))
NCHUNK = len(WIDTHS)
WMAX = max(WIDTHS)
SLOTS = 4
N_SEM = 320
MESH = pl.DeviceIdType.MESH
HI = lax.Precision.HIGHEST
F32 = jnp.float32
BF16 = jnp.bfloat16


def rot(base, step, size):
    return lax.rem(base + (step + size) % size, size)


def aligned(start, size, mult):
    return pl.ds(pl.multiple_of(start, mult), size)


def kernel(
    cot_hbm, act_hbm, nxt_hbm, w_hbm, row_old, col_old,
    w_out, s_out, q_out, rf_out, cf_out,
    rs_buf, cs_buf, cot, grad, w_buf, act, act_s, act_all, act_t, nxt, nxt_s, nxt_y, nxt_all,
    row_acc, row_send, row_recv, vec, vec_z, vec_xy, col_all, scal,
    w_own, w_peer, part, opp_send, opp_recv, x_send, x_recv, z_send, z_recv,
    local_sem, send_sem, recv_sem,
):
    dp = lax.axis_index("dp")
    mr = lax.axis_index("mrow")
    mc = lax.axis_index("mcol")
    x = lax.rem(mr, NX)
    y = lax.div(mr, NX)
    core = lax.rem(mc, 2)
    sib = {"mcol": mc + 1 - 2 * core}
    ymate = {"mrow": (1 - y) * NX + x}
    count = [0]
    sent = []

    def remote(src, dst, dev):
        i = count[0]
        count[0] += 1
        copy = pltpu.make_async_remote_copy(
            src_ref=src, dst_ref=dst, send_sem=send_sem.at[i], recv_sem=recv_sem.at[i],
            device_id=dev, device_id_type=MESH,
        )
        copy.start()
        sent.append(copy)
        return copy

    def zdev(k):
        return {"dp": rot(dp, k, NZ)}

    def pdev(k):
        place = rot(mr * 4 + mc, k, PLANE)
        return {"mrow": lax.div(place, 4), "mcol": lax.rem(place, 4)}

    def xdev(k):
        return {"mrow": y * NX + rot(x, k, NX)}

    def zrows(k, half=None):
        if half is None:
            return aligned(rot(dp, k, NZ) * TOK, TOK, 64)
        return aligned(rot(dp, k, NZ) * TOK + half * HALF, HALF, 32)

    loads = [
        pltpu.make_async_copy(act_hbm, act, local_sem.at[0]),
        pltpu.make_async_copy(cot_hbm, cot.at[zrows(0)], local_sem.at[1]),
        pltpu.make_async_copy(nxt_hbm, nxt, local_sem.at[2]),
        pltpu.make_async_copy(w_hbm, w_buf, local_sem.at[3]),
    ]
    for load in loads:
        load.start()

    barrier = pltpu.get_barrier_semaphore()
    for k in range(1, NZ):
        pl.semaphore_signal(barrier, inc=1, device_id=zdev(k), device_id_type=MESH)
    for k in range(1, PLANE):
        pl.semaphore_signal(barrier, inc=1, device_id=pdev(k), device_id_type=MESH)
    loads[0].wait()
    for k in range(NZ):
        act_s[k] = act[:, k * FEAT:(k + 1) * FEAT]
    loads[1].wait()
    loads[2].wait()
    for k in range(NZ):
        nxt_s[k] = nxt[:, k * FEAT:(k + 1) * FEAT]
    pl.semaphore_wait(barrier, NZ + PLANE - 2)

    q_rows = HALF // 2
    nxt_mate = remote(
        nxt_s.at[:, aligned((1 - y) * HALF + core * q_rows, q_rows, 16)], nxt_y, ymate
    )

    even = lax.rem(x, 2)
    flows = {
        "h": (H_BASE + (2 * y + even) * H_COLS, H_COLS),
        "b": (x * B_COLS, B_COLS),
        "e": (E_BASE + even * E_COLS, E_COLS // 2),
        "f": (E_BASE + even * E_COLS + E_COLS // 2, E_COLS // 2),
    }
    moves = {"h": (1 - 2 * even) * H_COLS, "e": (1 - 2 * even) * E_COLS}
    moves["f"] = moves["e"]
    z_in = {}

    def z_step(f, s):
        start, width = flows[f]
        cols = aligned(start, width, 128)
        for sign in (1, -1):
            half = None if s < 4 else (1 - sign) // 2
            ref = cot.at[zrows(-sign * (s - 1), half), cols]
            z_in[f, sign, s] = remote(ref, ref, zdev(sign))

    def z_next(f, s):
        for sign in (1, -1):
            z_in[f, sign, s].wait_recv()
        if s < 4:
            z_step(f, s + 1)

    def pieces(s):
        return (4,) if s == 4 else (-s, s)

    x_in = {}
    b_in = {}
    y_in = {}

    def x_ref(k, f, half):
        start, width = flows[f]
        return cot.at[zrows(k, half), aligned(start, width, 128)]

    def x_send_pair(f, k):
        for sign in (1, -1):
            ref = x_ref(k, f, (1 - sign) // 2)
            x_in[f, k, sign] = remote(ref, ref, xdev(sign))

    def b_direct(k):
        for sign in (1, -1):
            ref = x_ref(k, "b", None)
            x_in["b", k, sign] = remote(ref, ref, xdev(sign))

    def b_forward(k):
        for sign in (1, -1):
            x_in["b", k, sign].wait_recv()
            ref = cot.at[
                zrows(k, (1 - sign) // 2), aligned(rot(x, -sign, NX) * B_COLS, B_COLS, 128)
            ]
            b_in[k, sign] = remote(ref, ref, xdev(sign))

    def y_own(k):
        ref = x_ref(k, "h", None)
        y_in[k, 0] = remote(ref, ref, ymate)

    def y_other(k):
        for sign in (1, -1):
            x_in["h", k, sign].wait_recv()
        ref = cot.at[zrows(k), aligned(flows["h"][0] + moves["h"], H_COLS, 128)]
        y_in[k, 1] = remote(ref, ref, ymate)

    core_rows = aligned(core * HALF, HALF, 32)
    act_in = {}
    act_fwd = {}

    def act_forward(k):
        act_in[k].wait_recv()
        ref = act_all.at[zrows(-k, core)]
        act_fwd[k] = remote(ref, ref, sib)

    def act_send(k):
        act_in[k] = remote(
            act_s.at[rot(dp, k, NZ), core_rows], act_all.at[zrows(0, core)], zdev(k)
        )

    for f in ("h", "b", "e", "f"):
        z_step(f, 1)
    for s in range(1, 5):
        z_next("h", s)
        for k in pieces(s):
            x_send_pair("h", k)
            y_own(k)
        z_next("b", s)
        for k in pieces(s):
            b_direct(k)
        if s == 1:
            for k in (4, 3, 5):
                act_send(k)
            act_all[zrows(0), :] = act_s[dp]
            loads[3].wait()

            def weight_square(i, total):
                tile = w_buf[:, aligned(i * 256, 256, 256)]
                return total + jnp.sum((tile * tile).reshape(FEAT // 8, 8, 256), axis=0)

            wsq = lax.fori_loop(0, COLS // 256, weight_square, jnp.zeros((8, 256), F32))
            vec[...] = jnp.zeros((NZ, 8, 128), F32) + jnp.sum(wsq)
            row_acc[...] = jnp.zeros((FEAT, 128), F32)
        if s == 2:
            for k in (2, 6, 1, 7):
                act_send(k)
        if s > 1:
            for k in pieces(s - 1):
                y_other(k)
                b_forward(k)
        if s == 3:
            for k in (4, 3, 5):
                act_forward(k)
        if s == 4:
            for k in (2, 6, 1, 7):
                act_forward(k)
        for f in ("e", "f"):
            z_next(f, s)
            for k in pieces(s):
                x_send_pair(f, k)

    def nxt_part(z, j):
        return nxt_all.at[j, z, aligned(core * q_rows, q_rows, 16)]

    mine = aligned(y * HALF + core * q_rows, q_rows, 16)
    nxt_mate.wait_recv()
    nxt_in = {}
    for k in range(1, NZ):
        nxt_in[0, k] = remote(nxt_s.at[rot(dp, k, NZ), mine], nxt_part(dp, 0), zdev(k))
        nxt_in[1, k] = remote(nxt_y.at[rot(dp, k, NZ)], nxt_part(dp, 1), zdev(k))
    nxt_part(dp, 0)[...] = nxt_s[dp, mine, :]
    nxt_part(dp, 1)[...] = nxt_y[dp]

    for k in range(1, NZ):
        act_fwd[k].wait_recv()
    for i in range(4):
        rows = slice(i * 384, (i + 1) * 384)
        act_t[:, rows] = act_all[rows, :].T
    y_other(4)
    b_forward(4)

    def grad_tiles(base, tiles):
        def one(i, carry):
            start = base + i * 256
            cols = aligned(start, 256, 256)
            g = jnp.dot(act_t[...], cot[:, cols], preferred_element_type=F32)
            grad[:, cols] = g
            sq = g * g
            row_acc[...] += sq[:, :128] + sq[:, 128:]
            sums = jnp.sum(sq, axis=0, keepdims=True)
            for j in range(2):
                block = lax.div(start, 128) + j
                vec[lax.div(block, 3), pl.ds(lax.rem(block, 3), 1), :] = (
                    sums[:, j * 128:(j + 1) * 128]
                )
            return carry

        lax.fori_loop(0, tiles, one, 0)

    every = (-1, 1, -2, 2, -3, 3, 4)
    grad_tiles(H_BASE + y * 2 * H_COLS, 2 * H_COLS // 256)
    for k in every:
        for sign in (1, -1):
            b_in[k, sign].wait_recv()
    grad_tiles(0, NX * B_COLS // 256)
    grad_tiles(flows["e"][0], E_COLS // 256)
    for k in every:
        for j in range(2):
            y_in[k, j].wait_recv()
    grad_tiles(H_BASE + (1 - y) * 2 * H_COLS, 2 * H_COLS // 256)
    for k in every:
        for sign in (1, -1):
            x_in["e", k, sign].wait_recv()
            x_in["f", k, sign].wait_recv()
    grad_tiles(flows["e"][0] + moves["e"], E_COLS // 256)

    ones = jnp.ones((8, 128), F32)
    row_send[...] = lax.dot_general(
        ones, row_acc[...], (((1,), (1,)), ((), ())), precision=HI, preferred_element_type=F32
    )
    row_in = [
        remote(row_send, row_recv.at[k], {"mcol": rot(mc, k, 4)}) for k in range(1, 4)
    ]
    place = (mr * NZ + dp) * (FEAT // 32)
    first = lax.div(place, 4)
    shift = lax.rem(place, 4)
    near = jnp.concatenate([row_old[pl.ds(first + j, 1), :] for j in range(3)], axis=1)
    row_mine = near[:, 0:FEAT]
    for j in range(1, 4):
        row_mine = jnp.where(shift == j, near[:, j * 32:j * 32 + FEAT], row_mine)
    for copy in row_in:
        copy.wait_recv()
    row_full = ((row_send[...] + row_recv[1]) + row_recv[2]) + row_recv[3]
    row_factor = SECOND_DECAY * row_mine + (1.0 - SECOND_DECAY) * (
        row_full * (1.0 / QW) + SQUARE_EPS
    )
    rf_out[...] = row_factor[0:1]
    row_inv = lax.dot_general(
        1.0 / row_factor, ones * 0.125, (((0,), (0,)), ((), ())), precision=HI,
        preferred_element_type=F32,
    )

    def weighted(i, carry):
        g = grad[:, aligned(i * 256, 256, 256)]
        sums = jnp.sum(g * g * row_inv[:, 0:1], axis=0, keepdims=True)
        for j in range(2):
            block = i * 2 + j
            vec[lax.div(block, 3), pl.ds(3 + lax.rem(block, 3), 1), :] = (
                sums[:, j * 128:(j + 1) * 128]
            )
        return carry

    lax.fori_loop(0, COLS // 256, weighted, 0)

    sum_in = [
        remote(vec.at[rot(dp, k, NZ)], vec_z.at[k], zdev(k)) for k in range(1, NZ)
    ]
    total = vec[dp]
    for k in range(1, NZ):
        sum_in[k - 1].wait_recv()
        total = total + vec_z[k]
    vec_xy[0] = total
    sum_in = [
        remote(vec_xy.at[0], vec_xy.at[k], pdev(k)) for k in range(1, PLANE)
    ]
    old = []
    for d in range(4):
        base = rot(mc, -d, 4) * 24 + dp * 3
        old.append(jnp.concatenate(
            [col_old[pl.ds(base + j, 1), :] for j in range(3)], axis=0
        ))
    totals = [total, None, None, None]
    for k in range(1, PLANE):
        sum_in[k - 1].wait_recv()
    for k in range(1, PLANE):
        d = k % 4
        totals[d] = vec_xy[k] if totals[d] is None else totals[d] + vec_xy[k]
    square = jnp.zeros((3, 128), F32)
    moved = jnp.zeros((3, 128), F32)
    col_part = []
    for d in range(4):
        col_part.append(SECOND_DECAY * old[d] + (1.0 - SECOND_DECAY) * (
            totals[d][0:3] * (1.0 / D) + SQUARE_EPS
        ))
        square = square + totals[d][0:3]
        moved = moved + totals[d][3:6] / col_part[d]
    w_total = ((totals[0] + totals[1]) + totals[2]) + totals[3]
    scal[...] = jnp.zeros((8, 128), F32)
    scal[0:3] = col_part[0]
    scal[3:4] = jnp.sum(square, axis=0, keepdims=True)
    scal[4:5] = jnp.sum(moved, axis=0, keepdims=True)
    sum_in = [
        remote(scal, col_all.at[dp], zdev(k)) for k in range(1, NZ)
    ]
    col_all[dp] = scal[...]
    old_total = jnp.sum(row_old[...])
    row_root = jnp.sqrt(row_inv)
    for copy in sum_in:
        copy.wait_recv()
    sums = col_all[0]
    for k in range(1, NZ):
        sums = sums + col_all[k]
    for k in range(NZ):
        for j in range(3):
            cols = slice((k * 3 + j) * 128, (k * 3 + j + 1) * 128)
            cf_out[:, cols] = col_all[k, j:j + 1, :]
    cs_buf[...] = lax.rsqrt(cf_out[...])
    square_total = jnp.sum(sums[3:4], axis=1, keepdims=True)
    moved_total = jnp.sum(sums[4:5], axis=1, keepdims=True)
    row_mean = (
        SECOND_DECAY * old_total
        + (1.0 - SECOND_DECAY) * (square_total * (1.0 / QW) + D * SQUARE_EPS)
    ) * (1.0 / D)
    entries = float(D) * float(QW)
    clip = jnp.maximum(1.0, jnp.sqrt(row_mean * moved_total * (1.0 / entries)))
    w_scale = jnp.sqrt(w_total[6:7, 0:1] * (1.0 / entries))
    rs_buf[...] = row_root * (w_scale * jnp.sqrt(row_mean) / clip)

    w_in = []
    for c in range(NCHUNK):
        def update(i, carry, c=c):
            cols = aligned(STARTS[c] + i * 256, 256, 256)
            step = grad[:, cols] * (rs_buf[:, 0:1] * cs_buf[0:1, cols])
            new_w = w_buf[:, cols] - STEP_RATE * step
            grad[:, cols] = step
            w_buf[:, cols] = new_w
            w_own[:, cols] = new_w.astype(BF16)
            return carry

        lax.fori_loop(0, WIDTHS[c] // 256, update, 0)
        cols = pl.ds(STARTS[c], WIDTHS[c])
        w_in.append(remote(w_own.at[:, cols], w_peer.at[:, cols], ymate))
    outs = [
        pltpu.make_async_copy(w_buf, w_out, local_sem.at[4]),
        pltpu.make_async_copy(grad, s_out, local_sem.at[5]),
    ]
    for copy in outs:
        copy.start()
    nxt_fwd = []
    for j in range(2):
        for k in range(1, NZ):
            nxt_in[j, k].wait_recv()
        ref = nxt_all.at[j, :, aligned(core * q_rows, q_rows, 16)]
        nxt_fwd.append(remote(ref, ref, sib))
    for copy in nxt_fwd:
        copy.wait_recv()

    opp_in = {}
    q_in = {}
    z_part = {}
    x_next = rot(x, 1, NX)
    x_prev = rot(x, 3, NX)
    x_opp = rot(x, 2, NX)

    def block(c, q, lo, hi):
        return part[c % SLOTS, :, q, :, lo:hi].reshape(NZ * QTOK, hi - lo)

    def stage_matmul(c):
        w_in[c].wait_recv()
        width = WIDTHS[c]
        hw = width // 2

        def one(i, carry):
            src = aligned(STARTS[c] + i * 256, 256, 256)
            for r in range(2):
                zs = slice(r * 4, (r + 1) * 4)
                p = jnp.dot(
                    nxt_all[0, zs].reshape(4 * HALF, FEAT), w_own[:, src],
                    preferred_element_type=F32,
                )
                p = p + jnp.dot(
                    nxt_all[1, zs].reshape(4 * HALF, FEAT), w_peer[:, src],
                    preferred_element_type=F32,
                )
                part[c % SLOTS, zs, :, :, aligned(i * 256, 256, 256)] = (
                    p.reshape(4, NX, QTOK, 256)
                )
            return carry

        lax.fori_loop(0, width // 256, one, 0)
        cols = pl.ds(STARTS[c] // 2, hw)
        for j, sign in ((0, 1), (1, -1)):
            opp_send[j, :, cols] = block(c, x_opp, j * hw, (j + 1) * hw).astype(BF16)
            opp_in[c, j] = remote(
                opp_send.at[j, :, cols], opp_recv.at[j, :, cols], xdev(sign)
            )

    def stage_relay(c):
        width = WIDTHS[c]
        hw = width // 2
        base = STARTS[c]
        cols = pl.ds(base // 2, hw)
        for j, sign, q in ((0, 1, x_next), (1, -1, x_prev)):
            opp_in[c, j].wait_recv()
            lo = j * hw
            x_send[j, :, base + lo:base + lo + hw] = (
                block(c, q, lo, lo + hw) + opp_recv[j, :, cols].astype(F32)
            ).astype(BF16)
            lo = hw - lo
            x_send[j, :, base + lo:base + lo + hw] = block(c, q, lo, lo + hw).astype(BF16)
            full = pl.ds(base, width)
            q_in[c, j] = remote(x_send.at[j, :, full], x_recv.at[j, :, full], xdev(sign))

    def stage_z(c):
        width = WIDTHS[c]
        hw = width // 2
        base = STARTS[c]
        q_in[c, 0].wait_recv()
        q_in[c, 1].wait_recv()
        full = slice(base, base + width)
        summed = (
            block(c, x, 0, width)
            + x_recv[0, :, full].astype(F32) + x_recv[1, :, full].astype(F32)
        ).reshape(NZ, QTOK, width)
        part[c % SLOTS, :, x, :, 0:width] = summed
        cols = pl.ds(base // 2, hw)
        z_send[:, :, cols] = jnp.concatenate(
            [summed[:, :, :hw], summed[:, :, hw:]], axis=1
        ).astype(BF16)
        for k in range(1, NZ):
            z_part[c, k] = remote(
                z_send.at[rot(dp, k, NZ), :, cols], z_recv.at[k, :, cols], zdev(k)
            )
        q_out[:, full] = part[c % SLOTS, dp, x, :, 0:width]

    def stage_out(c):
        hw = WIDTHS[c] // 2
        acc = None
        for k in range(1, NZ):
            z_part[c, k].wait_recv()
            term = z_recv[k, :, pl.ds(STARTS[c] // 2, hw)].astype(F32)
            acc = term if acc is None else acc + term
        for j in range(2):
            cols = pl.ds(STARTS[c] + j * hw, hw)
            q_out[:, cols] = (q_out[:, cols] + acc[j * QTOK:(j + 1) * QTOK]) * D ** (-0.5)

    for t in range(NCHUNK):
        stage_matmul(t)
        if t >= 1:
            stage_relay(t - 1)
        if t >= 3:
            stage_z(t - 3)
        if t >= 5:
            stage_out(t - 5)
    stage_relay(NCHUNK - 1)
    for t in range(NCHUNK - 3, NCHUNK):
        stage_z(t)
    for t in range(NCHUNK - 5, NCHUNK):
        stage_out(t)

    for copy in outs:
        copy.wait()
    for copy in sent:
        copy.wait_send()
    assert count[0] <= N_SEM


def finish(*refs):
    src, dst, buf, sem = refs[:5], refs[5:10], refs[10:15], refs[15]
    views = []
    for i in range(2):
        for r in range(6):
            views.append((i, pl.ds(r * 48, 48)))
    views += [(i, slice(None)) for i in range(2, 5)]
    into = [
        pltpu.make_async_copy(src[i].at[rows], buf[i].at[rows], sem.at[0, n])
        for n, (i, rows) in enumerate(views)
    ]
    out = [
        pltpu.make_async_copy(buf[i].at[rows], dst[i].at[rows], sem.at[1, n])
        for n, (i, rows) in enumerate(views)
    ]
    for copy in into:
        copy.start()
    for first, second in zip(into, out):
        first.wait()
        second.start()
    for copy in out:
        copy.wait()


def body(weight, activations, cotangent, row_old, col_old, next_input):
    vm = pl.BlockSpec(memory_space=pltpu.VMEM)
    hbm = pl.BlockSpec(memory_space=pl.ANY)
    v = pltpu.VMEM

    def shape(*dims):
        return jax.ShapeDtypeStruct(dims, F32)

    new_weight, scaled_step, queries, row_factor, col_factor = pl.pallas_call(
        kernel,
        out_shape=(
            shape(FEAT, COLS), shape(FEAT, COLS), shape(QTOK, COLS), shape(1, FEAT),
            shape(1, COLS),
        ),
        in_specs=[hbm, hbm, hbm, hbm, vm, vm],
        out_specs=(hbm, hbm, vm, vm, vm),
        scratch_shapes=[
            v((FEAT, 128), F32),
            v((1, COLS), F32),
            v((TOKENS, COLS), BF16),
            v((FEAT, COLS), F32),
            v((FEAT, COLS), F32),
            v((TOK, BLOCK), BF16),
            v((NZ, TOK, FEAT), BF16),
            v((TOKENS, FEAT), BF16),
            v((FEAT, TOKENS), BF16),
            v((TOK, BLOCK), BF16),
            v((NZ, TOK, FEAT), BF16),
            v((NZ, HALF // 2, FEAT), BF16),
            v((2, NZ, HALF, FEAT), BF16),
            v((FEAT, 128), F32),
            v((8, FEAT), F32),
            v((4, 8, FEAT), F32),
            v((NZ, 8, 128), F32),
            v((NZ, 8, 128), F32),
            v((PLANE, 8, 128), F32),
            v((NZ, 8, 128), F32),
            v((8, 128), F32),
            v((FEAT, COLS), BF16),
            v((FEAT, COLS), BF16),
            v((SLOTS, NZ, NX, QTOK, WMAX), F32),
            v((2, TOK, COLS // 2), BF16),
            v((2, TOK, COLS // 2), BF16),
            v((2, TOK, COLS), BF16),
            v((2, TOK, COLS), BF16),
            v((NZ, 2 * QTOK, COLS // 2), BF16),
            v((NZ, 2 * QTOK, COLS // 2), BF16),
            pltpu.SemaphoreType.DMA((6,)),
            pltpu.SemaphoreType.DMA((N_SEM,)),
            pltpu.SemaphoreType.DMA((N_SEM,)),
        ],
        compiler_params=pltpu.CompilerParams(
            collective_id=0, has_side_effects=True, vmem_limit_bytes=60 * 1024 * 1024
        ),
        cost_estimate=pl.CostEstimate(
            flops=4 * TOKENS * FEAT * COLS, bytes_accessed=16_000_000, transcendentals=0
        ),
        name="update",
    )(
        cotangent, activations, next_input, weight,
        row_old.reshape(D // 128, 128), col_old.reshape(QW // 128, 128),
    )
    shapes = (
        shape(FEAT, COLS), shape(FEAT, COLS), shape(QTOK, COLS), shape(1, FEAT),
        shape(1, COLS),
    )
    new_weight, scaled_step, queries, row_factor, col_factor = pl.pallas_call(
        finish,
        in_specs=[hbm] * 5,
        out_specs=(hbm,) * 5,
        out_shape=shapes,
        scratch_shapes=[*(v(a.shape, F32) for a in shapes), pltpu.SemaphoreType.DMA((2, 15))],
        compiler_params=pltpu.CompilerParams(vmem_limit_bytes=60 * 1024 * 1024),
        cost_estimate=pl.CostEstimate(
            flops=0, bytes_accessed=16 * FEAT * COLS, transcendentals=0
        ),
        name="finish",
    )(new_weight, scaled_step, queries, row_factor, col_factor)
    return (
        new_weight, row_factor.reshape(FEAT), col_factor.reshape(COLS), queries, scaled_step,
    )


def solution(mesh):
    placed = (
        P(("mrow", "dp"), "mcol"),
        P("dp", "mrow"),
        P("dp", "mcol"),
        P(),
        P(),
        P("dp", "mrow"),
    )
    return jax.shard_map(
        body,
        mesh=mesh,
        in_specs=placed,
        out_specs=(
            P(("mrow", "dp"), "mcol"),
            P(("mrow", "dp")),
            P("mcol"),
            P(("dp", "mrow"), "mcol"),
            P(("mrow", "dp"), "mcol"),
        ),
        check_vma=False,
    )
```

time: 852 us -> 164 us (0.19)
  waiting for transfers between devices: 713 us -> 0 us
  Pallas kernels: 0 us -> 162 us
  blocking collectives: 73.1 us -> 0 us
  other arithmetic: 23.3 us -> 1.27 us
  matrix products: 21.9 us -> 0 us
  between operations: 16.5 us -> 0.65 us
    reduce_scatter x2 -> x0, waiting for transfers between devices: 329 us -> none  [the longest x1 285 us: body(): lax.psum_scatter(lax.dot_general(inputs, cotangent, (((0,), (0,)), ((), (...]
    psum x1 -> x0, waiting for transfers between devices: 238 us -> none  [body(): summed = lax.psum(vector, ('dp', 'mrow', 'mcol'))]
    pallas_call x0 -> x2, Pallas kernels: none -> 162 us  [the longest x1 156 us: body(): pl.pallas_call(kernel, out_shape=(shape(FEAT, COLS), shape(FEAT, COLS), s...]
    all_gather x1 -> x0, waiting for transfers between devices: 146 us -> none  [body(): lax.all_gather(weight_half, 'dp', axis=0, tiled=True)]
    psum x1 -> x0, blocking collectives: 73.1 us -> none  [body(): lax.psum((jnp.sum(direction * direction), jnp.sum(weight * weight)), ('dp...]
    dot_general x2 -> x0, matrix products: 22 us -> none  [the longest x1 12.5 us: body(): lax.dot_general(inputs, cotangent, (((0,), (0,)), ((), ())), preferred_el...]
    reduce_sum x5 -> x0, other arithmetic: 11.7 us -> none  [the longest x1 3.6 us: body(): jnp.sum(direction * direction)]
  transfers between devices with their start and end apart: 4 -> 0, of which waited for: 4 -> 0; matrix products, arithmetic and copies ran while one was open for 0% -> 0% of each run, Pallas kernels for 0% -> 0%
where the time goes in v2:
time: 164 us
  Pallas kernels  162 us (99%)
    pallas_call x1, Pallas kernels, body(): pl.pallas_call(kernel, out_shape=(shape(FEAT, COLS), shape(FEAT, COLS), s...  156 us
    pallas_call x1, Pallas kernels, body(): pl.pallas_call(finish, in_specs=[hbm] * 5, out_specs=(hbm,) * 5, out_shap...  5.95 us

profile of v2, /device:TPU:8, one launch (start us, length us, event | category | flops | bytes accessed | tf_op | source)
XLA Modules:
  0.0 164.1 jit_solution(1197421243835876850)
XLA Ops:
  0.6 156.2 %update.1 = (f32[288,3072]{1,0:T(8,128)}, f32[288,3072]{1,0:T(8,128)}, f32[24,3072]{1,0:T(8,128)}, f32[1,288]{1,0:T(1,128)}, f32[1,3072]{1,0:T(1,128)}) custom-call(bf16[192,3072]{1,0:T(8,128)(2,1)} %cot_hbm.1, bf16[192,2304]{1,0:T(8,128)(2,1)} %act_hbm.1, bf16[192,2304]{1,0:T(8,128)(2,1)} %nxt_hbm.1, f32[288,3072]{1,0:T(8,128)} %w_hbm.1, ...), custom_call_target="tpu_custom_call" | custom-call | flops 5435817984 | bytes 16000000 | tf_op jit(solution)/shard_map/update/pallas_call | solution.py:569
  156.9 5.9 %finish.1 = (f32[288,3072]{1,0:T(8,128)}, f32[288,3072]{1,0:T(8,128)}, f32[24,3072]{1,0:T(8,128)}, f32[1,288]{1,0:T(1,128)}, f32[1,3072]{1,0:T(1,128)}) custom-call(f32[288,3072]{1,0:T(8,128)} %get-tuple-element.15.refs_0_, f32[288,3072]{1,0:T(8,128)} %get-tuple-element.16.refs_1_, f32[24,3072]{1,0:T(8,128)} %get-tuple-element.17.refs_2_, ...), custom_call_target="tpu_custom_call" | custom-call | bytes 14155776 | tf_op jit(solution)/shard_map/finish/pallas_call | solution.py:627
  162.8 1.3 reduce

commit v3 on v2

--- a/solution.py
+++ b/solution.py
@@ -26,12 +26,12 @@
 E_COLS = 768
 H_BASE = 2048
 H_COLS = 256
-WIDTHS = (256, 256, 512, 512, 512, 512, 256, 256)
+WIDTHS = (256,) * 12
 STARTS = tuple(sum(WIDTHS[:i]) for i in range(len(WIDTHS)))
 NCHUNK = len(WIDTHS)
 WMAX = max(WIDTHS)
 SLOTS = 4
-N_SEM = 320
+N_SEM = 384
 MESH = pl.DeviceIdType.MESH
 HI = lax.Precision.HIGHEST
 F32 = jnp.float32
@@ -114,11 +114,6 @@
         nxt_s[k] = nxt[:, k * FEAT:(k + 1) * FEAT]
     pl.semaphore_wait(barrier, NZ + PLANE - 2)
 
-    q_rows = HALF // 2
-    nxt_mate = remote(
-        nxt_s.at[:, aligned((1 - y) * HALF + core * q_rows, q_rows, 16)], nxt_y, ymate
-    )
-
     even = lax.rem(x, 2)
     flows = {
         "h": (H_BASE + (2 * y + even) * H_COLS, H_COLS),
@@ -183,19 +178,29 @@
         ref = cot.at[zrows(k), aligned(flows["h"][0] + moves["h"], H_COLS, 128)]
         y_in[k, 1] = remote(ref, ref, ymate)
 
-    core_rows = aligned(core * HALF, HALF, 32)
+    quarter = core * HALF + lax.div(mc, 2) * (HALF // 2)
     act_in = {}
+    act_mid = {}
     act_fwd = {}
 
+    def act_rows(k):
+        return aligned(rot(dp, k, NZ) * TOK + quarter, HALF // 2, 16)
+
+    def act_send(k):
+        act_in[k] = remote(
+            act_s.at[rot(dp, k, NZ), aligned(quarter, HALF // 2, 16)],
+            act_all.at[act_rows(0)], zdev(k),
+        )
+
+    def act_middle(k):
+        act_in[k].wait_recv()
+        ref = act_all.at[act_rows(-k)]
+        act_mid[k] = remote(ref, ref, {"mcol": rot(mc, 2, 4)})
+
     def act_forward(k):
-        act_in[k].wait_recv()
+        act_mid[k].wait_recv()
         ref = act_all.at[zrows(-k, core)]
         act_fwd[k] = remote(ref, ref, sib)
-
-    def act_send(k):
-        act_in[k] = remote(
-            act_s.at[rot(dp, k, NZ), core_rows], act_all.at[zrows(0, core)], zdev(k)
-        )
 
     for f in ("h", "b", "e", "f"):
         z_step(f, 1)
@@ -227,36 +232,45 @@
             for k in pieces(s - 1):
                 y_other(k)
                 b_forward(k)
+        if s == 2:
+            for k in (4, 3, 5):
+                act_middle(k)
         if s == 3:
-            for k in (4, 3, 5):
-                act_forward(k)
+            for k in (2, 6, 1, 7):
+                act_middle(k)
         if s == 4:
-            for k in (2, 6, 1, 7):
+            for k in (4, 3, 5, 2, 6, 1, 7):
                 act_forward(k)
         for f in ("e", "f"):
             z_next(f, s)
             for k in pieces(s):
                 x_send_pair(f, k)
 
+    q_rows = HALF // 2
+
     def nxt_part(z, j):
         return nxt_all.at[j, z, aligned(core * q_rows, q_rows, 16)]
 
     mine = aligned(y * HALF + core * q_rows, q_rows, 16)
-    nxt_mate.wait_recv()
     nxt_in = {}
-    for k in range(1, NZ):
-        nxt_in[0, k] = remote(nxt_s.at[rot(dp, k, NZ), mine], nxt_part(dp, 0), zdev(k))
-        nxt_in[1, k] = remote(nxt_y.at[rot(dp, k, NZ)], nxt_part(dp, 1), zdev(k))
-    nxt_part(dp, 0)[...] = nxt_s[dp, mine, :]
-    nxt_part(dp, 1)[...] = nxt_y[dp]
-
+
+    def nxt_send(j):
+        for k in range(1, NZ):
+            src = nxt_s.at[rot(dp, k, NZ), mine] if j == 0 else nxt_y.at[rot(dp, k, NZ)]
+            nxt_in[j, k] = remote(src, nxt_part(dp, j), zdev(k))
+        nxt_part(dp, j)[...] = nxt_s[dp, mine, :] if j == 0 else nxt_y[dp]
+
+    y_other(4)
+    b_forward(4)
+    nxt_send(0)
+    nxt_mate = remote(
+        nxt_s.at[:, aligned((1 - y) * HALF + core * q_rows, q_rows, 16)], nxt_y, ymate
+    )
     for k in range(1, NZ):
         act_fwd[k].wait_recv()
     for i in range(4):
         rows = slice(i * 384, (i + 1) * 384)
         act_t[:, rows] = act_all[rows, :].T
-    y_other(4)
-    b_forward(4)
 
     def grad_tiles(base, tiles):
         def one(i, carry):
@@ -313,19 +327,18 @@
     row_factor = SECOND_DECAY * row_mine + (1.0 - SECOND_DECAY) * (
         row_full * (1.0 / QW) + SQUARE_EPS
     )
-    rf_out[...] = row_factor[0:1]
+    rf_out[...] = row_factor[0]
     row_inv = lax.dot_general(
         1.0 / row_factor, ones * 0.125, (((0,), (0,)), ((), ())), precision=HI,
         preferred_element_type=F32,
     )
 
     def weighted(i, carry):
-        g = grad[:, aligned(i * 256, 256, 256)]
-        sums = jnp.sum(g * g * row_inv[:, 0:1], axis=0, keepdims=True)
         for j in range(2):
             block = i * 2 + j
+            g = grad[:, aligned(block * 128, 128, 128)]
             vec[lax.div(block, 3), pl.ds(3 + lax.rem(block, 3), 1), :] = (
-                sums[:, j * 128:(j + 1) * 128]
+                jnp.sum(g * g * row_inv, axis=0, keepdims=True)
             )
         return carry
 
@@ -372,6 +385,8 @@
         remote(scal, col_all.at[dp], zdev(k)) for k in range(1, NZ)
     ]
     col_all[dp] = scal[...]
+    nxt_mate.wait_recv()
+    nxt_send(1)
     old_total = jnp.sum(row_old[...])
     row_root = jnp.sqrt(row_inv)
     for copy in sum_in:
@@ -398,15 +413,15 @@
     w_in = []
     for c in range(NCHUNK):
         def update(i, carry, c=c):
-            cols = aligned(STARTS[c] + i * 256, 256, 256)
-            step = grad[:, cols] * (rs_buf[:, 0:1] * cs_buf[0:1, cols])
+            cols = aligned(STARTS[c] + i * 128, 128, 128)
+            step = grad[:, cols] * (rs_buf[...] * cs_buf[0:1, cols])
             new_w = w_buf[:, cols] - STEP_RATE * step
             grad[:, cols] = step
             w_buf[:, cols] = new_w
             w_own[:, cols] = new_w.astype(BF16)
             return carry
 
-        lax.fori_loop(0, WIDTHS[c] // 256, update, 0)
+        lax.fori_loop(0, WIDTHS[c] // 128, update, 0)
         cols = pl.ds(STARTS[c], WIDTHS[c])
         w_in.append(remote(w_own.at[:, cols], w_peer.at[:, cols], ymate))
     outs = [
@@ -461,7 +476,8 @@
         for j, sign in ((0, 1), (1, -1)):
             opp_send[j, :, cols] = block(c, x_opp, j * hw, (j + 1) * hw).astype(BF16)
             opp_in[c, j] = remote(
-                opp_send.at[j, :, cols], opp_recv.at[j, :, cols], xdev(sign)
+                opp_send.at[j, :, cols], opp_recv.at[j, :, cols],
+                xdev(sign),
             )
 
     def stage_relay(c):
@@ -569,7 +585,7 @@
     new_weight, scaled_step, queries, row_factor, col_factor = pl.pallas_call(
         kernel,
         out_shape=(
-            shape(FEAT, COLS), shape(FEAT, COLS), shape(QTOK, COLS), shape(1, FEAT),
+            shape(FEAT, COLS), shape(FEAT, COLS), shape(QTOK, COLS), shape(FEAT),
             shape(1, COLS),
         ),
         in_specs=[hbm, hbm, hbm, hbm, vm, vm],
@@ -621,7 +637,7 @@
         row_old.reshape(D // 128, 128), col_old.reshape(QW // 128, 128),
     )
     shapes = (
-        shape(FEAT, COLS), shape(FEAT, COLS), shape(QTOK, COLS), shape(1, FEAT),
+        shape(FEAT, COLS), shape(FEAT, COLS), shape(QTOK, COLS), shape(FEAT),
         shape(1, COLS),
     )
     new_weight, scaled_step, queries, row_factor, col_factor = pl.pallas_call(
@@ -637,7 +653,7 @@
         name="finish",
     )(new_weight, scaled_step, queries, row_factor, col_factor)
     return (
-        new_weight, row_factor.reshape(FEAT), col_factor.reshape(COLS), queries, scaled_step,
+        new_weight, row_factor, col_factor.reshape(COLS), queries, scaled_step,
     )
 
 

time: 164 us -> 153 us (0.933)
  Pallas kernels: 162 us -> 152 us
    pallas_call x1, Pallas kernels: 156 us -> 146 us  [body(): pl.pallas_call(kernel, out_shape=(shape(FEAT, COLS), shape(FEAT, COLS), s...]
where the time goes in v3:
time: 153 us
  Pallas kernels  152 us (99%)
    pallas_call x1, Pallas kernels, body(): pl.pallas_call(kernel, out_shape=(shape(FEAT, COLS), shape(FEAT, COLS), s...  146 us
    pallas_call x1, Pallas kernels, body(): pl.pallas_call(finish, in_specs=[hbm] * 5, out_specs=(hbm,) * 5, out_shap...  5.95 us

profile of v3, /device:TPU:8, one launch (start us, length us, event | category | flops | bytes accessed | tf_op | source)
XLA Modules:
  0.0 153.0 jit_solution(7650884368388876409)
XLA Ops:
  0.6 146.4 %update.1 = (f32[288,3072]{1,0:T(8,128)}, f32[288,3072]{1,0:T(8,128)}, f32[24,3072]{1,0:T(8,128)}, f32[288]{0:T(512)}, f32[1,3072]{1,0:T(1,128)}) custom-call(bf16[192,3072]{1,0:T(8,128)(2,1)} %cot_hbm.1, bf16[192,2304]{1,0:T(8,128)(2,1)} %act_hbm.1, bf16[192,2304]{1,0:T(8,128)(2,1)} %nxt_hbm.1, f32[288,3072]{1,0:T(8,128)} %w_hbm.1, f32[144,128]{1,0:T(8,128)} %bitcast.3, ...), custom_call_target="tpu_custom_call" | custom-call | flops 5435817984 | bytes 16000000 | tf_op jit(solution)/shard_map/update/pallas_call | solution.py:585
  147.1 5.9 %finish.1 = (f32[288,3072]{1,0:T(8,128)}, f32[288,3072]{1,0:T(8,128)}, f32[24,3072]{1,0:T(8,128)}, f32[288]{0:T(512)}, f32[1,3072]{1,0:T(1,128)}) custom-call(f32[288,3072]{1,0:T(8,128)} %get-tuple-element.15.refs_0_, f32[288,3072]{1,0:T(8,128)} %get-tuple-element.16.refs_1_, f32[24,3072]{1,0:T(8,128)} %get-tuple-element.17.refs_2_, ...), custom_call_target="tpu_custom_call" | custom-call | bytes 14155776 | tf_op jit(solution)/shard_map/finish/pallas_call | solution.py:643

commit v4 on v3

--- a/solution.py
+++ b/solution.py
@@ -31,6 +31,10 @@
 NCHUNK = len(WIDTHS)
 WMAX = max(WIDTHS)
 SLOTS = 4
+ORDER = (0, -1, 1, -2, 2, -3, 3, 4)
+SLOT = {k % NZ: i for i, k in enumerate(ORDER)}
+EARLY = 5 * TOK
+LATE = TOKENS - EARLY
 N_SEM = 384
 MESH = pl.DeviceIdType.MESH
 HI = lax.Precision.HIGHEST
@@ -49,9 +53,9 @@
 def kernel(
     cot_hbm, act_hbm, nxt_hbm, w_hbm, row_old, col_old,
     w_out, s_out, q_out, rf_out, cf_out,
-    rs_buf, cs_buf, cot, grad, w_buf, act, act_s, act_all, act_t, nxt, nxt_s, nxt_y, nxt_all,
+    rs_buf, cs_buf, cot, grad, w_buf, act, act_s, act_all, act_t, act_u, nxt, nxt_s, nxt_y, nxt_all,
     row_acc, row_send, row_recv, vec, vec_z, vec_xy, col_all, scal,
-    w_own, w_peer, part, opp_send, opp_recv, x_send, x_recv, z_send, z_recv,
+    w_mate, g_mate, row_own, row_mate, w_own, w_peer, part, opp_send, opp_recv, x_send, x_recv, z_send, z_recv,
     local_sem, send_sem, recv_sem,
 ):
     dp = lax.axis_index("dp")
@@ -65,7 +69,7 @@
     count = [0]
     sent = []
 
-    def remote(src, dst, dev):
+    def remote(src, dst, dev, late=True):
         i = count[0]
         count[0] += 1
         copy = pltpu.make_async_remote_copy(
@@ -73,7 +77,8 @@
             device_id=dev, device_id_type=MESH,
         )
         copy.start()
-        sent.append(copy)
+        if late:
+            sent.append(copy)
         return copy
 
     def zdev(k):
@@ -87,9 +92,12 @@
         return {"mrow": y * NX + rot(x, k, NX)}
 
     def zrows(k, half=None):
+        first = SLOT[k % NZ] * TOK
         if half is None:
-            return aligned(rot(dp, k, NZ) * TOK, TOK, 64)
-        return aligned(rot(dp, k, NZ) * TOK + half * HALF, HALF, 32)
+            return pl.ds(first, TOK)
+        if isinstance(half, int):
+            return pl.ds(first + half * HALF, HALF)
+        return aligned(first + half * HALF, HALF, 32)
 
     loads = [
         pltpu.make_async_copy(act_hbm, act, local_sem.at[0]),
@@ -112,6 +120,7 @@
     loads[2].wait()
     for k in range(NZ):
         nxt_s[k] = nxt[:, k * FEAT:(k + 1) * FEAT]
+    loads[3].wait()
     pl.semaphore_wait(barrier, NZ + PLANE - 2)
 
     even = lax.rem(x, 2)
@@ -130,8 +139,9 @@
         cols = aligned(start, width, 128)
         for sign in (1, -1):
             half = None if s < 4 else (1 - sign) // 2
-            ref = cot.at[zrows(-sign * (s - 1), half), cols]
-            z_in[f, sign, s] = remote(ref, ref, zdev(sign))
+            src = cot.at[zrows(-sign * (s - 1), half), cols]
+            dst = cot.at[zrows(-sign * s, half), cols]
+            z_in[f, sign, s] = remote(src, dst, zdev(sign))
 
     def z_next(f, s):
         for sign in (1, -1):
@@ -184,12 +194,12 @@
     act_fwd = {}
 
     def act_rows(k):
-        return aligned(rot(dp, k, NZ) * TOK + quarter, HALF // 2, 16)
+        return aligned(SLOT[k % NZ] * TOK + quarter, HALF // 2, 16)
 
     def act_send(k):
         act_in[k] = remote(
             act_s.at[rot(dp, k, NZ), aligned(quarter, HALF // 2, 16)],
-            act_all.at[act_rows(0)], zdev(k),
+            act_all.at[act_rows(-k)], zdev(k),
         )
 
     def act_middle(k):
@@ -202,21 +212,30 @@
         ref = act_all.at[zrows(-k, core)]
         act_fwd[k] = remote(ref, ref, sib)
 
-    for f in ("h", "b", "e", "f"):
+    for f in ("b", "h", "e", "f"):
         z_step(f, 1)
+    early = pl.ds(STARTS[0], WIDTHS[0])
+    q_rows = HALF // 2
+    nxt_mate = remote(
+        nxt_s.at[:, aligned((1 - y) * HALF + core * q_rows, q_rows, 16)], nxt_y, ymate
+    )
     for s in range(1, 5):
+        if s == 1:
+            z_next("b", s)
+            for k in pieces(s):
+                b_direct(k)
         z_next("h", s)
         for k in pieces(s):
             x_send_pair("h", k)
             y_own(k)
-        z_next("b", s)
-        for k in pieces(s):
-            b_direct(k)
+        if s > 1:
+            z_next("b", s)
+            for k in pieces(s):
+                b_direct(k)
         if s == 1:
             for k in (4, 3, 5):
                 act_send(k)
             act_all[zrows(0), :] = act_s[dp]
-            loads[3].wait()
 
             def weight_square(i, total):
                 tile = w_buf[:, aligned(i * 256, 256, 256)]
@@ -246,8 +265,6 @@
             for k in pieces(s):
                 x_send_pair(f, k)
 
-    q_rows = HALF // 2
-
     def nxt_part(z, j):
         return nxt_all.at[j, z, aligned(core * q_rows, q_rows, 16)]
 
@@ -263,20 +280,25 @@
     y_other(4)
     b_forward(4)
     nxt_send(0)
-    nxt_mate = remote(
-        nxt_s.at[:, aligned((1 - y) * HALF + core * q_rows, q_rows, 16)], nxt_y, ymate
-    )
+    nxt_mate.wait_recv()
+    nxt_send(1)
+    mate_w = remote(w_buf.at[:, early], w_mate, ymate, late=False)
     for k in range(1, NZ):
         act_fwd[k].wait_recv()
-    for i in range(4):
-        rows = slice(i * 384, (i + 1) * 384)
+    for i in (0, 384, 768):
+        rows = slice(i, min(i + 384, EARLY))
         act_t[:, rows] = act_all[rows, :].T
+    for i in (0, 384):
+        rows = slice(i, min(i + 384, LATE))
+        act_u[:, rows] = act_all[EARLY + rows.start:EARLY + rows.stop, :].T
 
     def grad_tiles(base, tiles):
         def one(i, carry):
             start = base + i * 256
             cols = aligned(start, 256, 256)
-            g = jnp.dot(act_t[...], cot[:, cols], preferred_element_type=F32)
+            g = grad[:, cols] + jnp.dot(
+                act_u[...], cot[EARLY:TOKENS, cols], preferred_element_type=F32
+            )
             grad[:, cols] = g
             sq = g * g
             row_acc[...] += sq[:, :128] + sq[:, 128:]
@@ -290,7 +312,20 @@
 
         lax.fori_loop(0, tiles, one, 0)
 
-    every = (-1, 1, -2, 2, -3, 3, 4)
+    def grad_early(i, carry):
+        cols = aligned(i * 256, 256, 256)
+        grad[:, cols] = jnp.dot(act_t[...], cot[0:EARLY, cols], preferred_element_type=F32)
+        return carry
+
+    for k in ORDER[1:5]:
+        for sign in (1, -1):
+            b_in[k, sign].wait_recv()
+            x_in["e", k, sign].wait_recv()
+            x_in["f", k, sign].wait_recv()
+        for j in range(2):
+            y_in[k, j].wait_recv()
+    lax.fori_loop(0, COLS // 256, grad_early, 0)
+    every = ORDER[5:]
     grad_tiles(H_BASE + y * 2 * H_COLS, 2 * H_COLS // 256)
     for k in every:
         for sign in (1, -1):
@@ -314,6 +349,7 @@
     row_in = [
         remote(row_send, row_recv.at[k], {"mcol": rot(mc, k, 4)}) for k in range(1, 4)
     ]
+    mate_g = remote(grad.at[:, early], g_mate, ymate, late=False)
     place = (mr * NZ + dp) * (FEAT // 32)
     first = lax.div(place, 4)
     shift = lax.rem(place, 4)
@@ -328,6 +364,8 @@
         row_full * (1.0 / QW) + SQUARE_EPS
     )
     rf_out[...] = row_factor[0]
+    row_own[...] = row_factor
+    mate_r = remote(row_own, row_mate, ymate)
     row_inv = lax.dot_general(
         1.0 / row_factor, ones * 0.125, (((0,), (0,)), ((), ())), precision=HI,
         preferred_element_type=F32,
@@ -385,8 +423,12 @@
         remote(scal, col_all.at[dp], zdev(k)) for k in range(1, NZ)
     ]
     col_all[dp] = scal[...]
-    nxt_mate.wait_recv()
-    nxt_send(1)
+    nxt_fwd = []
+    for j in range(2):
+        for k in range(1, NZ):
+            nxt_in[j, k].wait_recv()
+        ref = nxt_all.at[j, :, aligned(core * q_rows, q_rows, 16)]
+        nxt_fwd.append(remote(ref, ref, sib))
     old_total = jnp.sum(row_old[...])
     row_root = jnp.sqrt(row_inv)
     for copy in sum_in:
@@ -408,10 +450,22 @@
     entries = float(D) * float(QW)
     clip = jnp.maximum(1.0, jnp.sqrt(row_mean * moved_total * (1.0 / entries)))
     w_scale = jnp.sqrt(w_total[6:7, 0:1] * (1.0 / entries))
-    rs_buf[...] = row_root * (w_scale * jnp.sqrt(row_mean) / clip)
-
+    scale = w_scale * jnp.sqrt(row_mean) / clip
+    rs_buf[...] = row_root * scale
+
+    mate_w.wait()
+    mate_g.wait()
+    mate_r.wait_recv()
+    mate_scale = scale * jnp.sqrt(lax.dot_general(
+        1.0 / row_mate[...], ones * 0.125, (((0,), (0,)), ((), ())), precision=HI,
+        preferred_element_type=F32,
+    ))
+    for i in range(WIDTHS[0] // 128):
+        cols = slice(i * 128, (i + 1) * 128)
+        step = g_mate[:, cols] * (mate_scale * cs_buf[0:1, cols])
+        w_peer[:, cols] = (w_mate[:, cols] - STEP_RATE * step).astype(BF16)
     w_in = []
-    for c in range(NCHUNK):
+    for c in (*range(1, NCHUNK), 0):
         def update(i, carry, c=c):
             cols = aligned(STARTS[c] + i * 128, 128, 128)
             step = grad[:, cols] * (rs_buf[...] * cs_buf[0:1, cols])
@@ -422,20 +476,15 @@
             return carry
 
         lax.fori_loop(0, WIDTHS[c] // 128, update, 0)
-        cols = pl.ds(STARTS[c], WIDTHS[c])
-        w_in.append(remote(w_own.at[:, cols], w_peer.at[:, cols], ymate))
+        if c > 0:
+            cols = pl.ds(STARTS[c], WIDTHS[c])
+            w_in.append(remote(w_own.at[:, cols], w_peer.at[:, cols], ymate))
     outs = [
         pltpu.make_async_copy(w_buf, w_out, local_sem.at[4]),
         pltpu.make_async_copy(grad, s_out, local_sem.at[5]),
     ]
     for copy in outs:
         copy.start()
-    nxt_fwd = []
-    for j in range(2):
-        for k in range(1, NZ):
-            nxt_in[j, k].wait_recv()
-        ref = nxt_all.at[j, :, aligned(core * q_rows, q_rows, 16)]
-        nxt_fwd.append(remote(ref, ref, sib))
     for copy in nxt_fwd:
         copy.wait_recv()
 
@@ -450,7 +499,8 @@
         return part[c % SLOTS, :, q, :, lo:hi].reshape(NZ * QTOK, hi - lo)
 
     def stage_matmul(c):
-        w_in[c].wait_recv()
+        if c > 0:
+            w_in[c - 1].wait_recv()
         width = WIDTHS[c]
         hw = width // 2
 
@@ -599,7 +649,8 @@
             v((TOK, BLOCK), BF16),
             v((NZ, TOK, FEAT), BF16),
             v((TOKENS, FEAT), BF16),
-            v((FEAT, TOKENS), BF16),
+            v((FEAT, EARLY), BF16),
+            v((FEAT, LATE), BF16),
             v((TOK, BLOCK), BF16),
             v((NZ, TOK, FEAT), BF16),
             v((NZ, HALF // 2, FEAT), BF16),
@@ -612,6 +663,10 @@
             v((PLANE, 8, 128), F32),
             v((NZ, 8, 128), F32),
             v((8, 128), F32),
+            v((FEAT, WIDTHS[0]), F32),
+            v((FEAT, WIDTHS[0]), F32),
+            v((8, FEAT), F32),
+            v((8, FEAT), F32),
             v((FEAT, COLS), BF16),
             v((FEAT, COLS), BF16),
             v((SLOTS, NZ, NX, QTOK, WMAX), F32),

time: 153 us -> 150 us (0.980)
  Pallas kernels: 152 us -> 149 us
    pallas_call x1, Pallas kernels: 146 us -> 143 us  [body(): pl.pallas_call(kernel, out_shape=(shape(FEAT, COLS), shape(FEAT, COLS), s...]
where the time goes in v4:
time: 150 us
  Pallas kernels  149 us (99%)
    pallas_call x1, Pallas kernels, body(): pl.pallas_call(kernel, out_shape=(shape(FEAT, COLS), shape(FEAT, COLS), s...  143 us
    pallas_call x1, Pallas kernels, body(): pl.pallas_call(finish, in_specs=[hbm] * 5, out_specs=(hbm,) * 5, out_shap...  5.95 us

profile of v4, /device:TPU:8, one launch (start us, length us, event | category | flops | bytes accessed | tf_op | source)
XLA Modules:
  0.0 150.0 jit_solution(12978752903530665550)
XLA Ops:
  0.6 143.4 %update.1 = (f32[288,3072]{1,0:T(8,128)}, f32[288,3072]{1,0:T(8,128)}, f32[24,3072]{1,0:T(8,128)}, f32[288]{0:T(512)}, f32[1,3072]{1,0:T(1,128)}) custom-call(bf16[192,3072]{1,0:T(8,128)(2,1)} %cot_hbm.1, bf16[192,2304]{1,0:T(8,128)(2,1)} %act_hbm.1, bf16[192,2304]{1,0:T(8,128)(2,1)} %nxt_hbm.1, f32[288,3072]{1,0:T(8,128)} %w_hbm.1, f32[144,128]{1,0:T(8,128)} %bitcast.3, ...), custom_call_target="tpu_custom_call" | custom-call | flops 5435817984 | bytes 16000000 | tf_op jit(solution)/shard_map/update/pallas_call | solution.py:635
  144.1 5.9 %finish.1 = (f32[288,3072]{1,0:T(8,128)}, f32[288,3072]{1,0:T(8,128)}, f32[24,3072]{1,0:T(8,128)}, f32[288]{0:T(512)}, f32[1,3072]{1,0:T(1,128)}) custom-call(f32[288,3072]{1,0:T(8,128)} %get-tuple-element.15.refs_0_, f32[288,3072]{1,0:T(8,128)} %get-tuple-element.16.refs_1_, f32[24,3072]{1,0:T(8,128)} %get-tuple-element.17.refs_2_, ...), custom_call_target="tpu_custom_call" | custom-call | bytes 14155776 | tf_op jit(solution)/shard_map/finish/pallas_call | solution.py:698

commit v5 on v4

--- a/solution.py
+++ b/solution.py
@@ -465,8 +465,9 @@
         step = g_mate[:, cols] * (mate_scale * cs_buf[0:1, cols])
         w_peer[:, cols] = (w_mate[:, cols] - STEP_RATE * step).astype(BF16)
     w_in = []
-    for c in (*range(1, NCHUNK), 0):
-        def update(i, carry, c=c):
+
+    def refresh(c):
+        def update(i, carry):
             cols = aligned(STARTS[c] + i * 128, 128, 128)
             step = grad[:, cols] * (rs_buf[...] * cs_buf[0:1, cols])
             new_w = w_buf[:, cols] - STEP_RATE * step
@@ -479,12 +480,9 @@
         if c > 0:
             cols = pl.ds(STARTS[c], WIDTHS[c])
             w_in.append(remote(w_own.at[:, cols], w_peer.at[:, cols], ymate))
-    outs = [
-        pltpu.make_async_copy(w_buf, w_out, local_sem.at[4]),
-        pltpu.make_async_copy(grad, s_out, local_sem.at[5]),
-    ]
-    for copy in outs:
-        copy.start()
+
+    for c in (1, 2, 3, 0):
+        refresh(c)
     for copy in nxt_fwd:
         copy.wait_recv()
 
@@ -581,6 +579,15 @@
 
     for t in range(NCHUNK):
         stage_matmul(t)
+        if t == 0:
+            for c in range(4, NCHUNK):
+                refresh(c)
+            outs = [
+                pltpu.make_async_copy(w_buf, w_out, local_sem.at[4]),
+                pltpu.make_async_copy(grad, s_out, local_sem.at[5]),
+            ]
+            for copy in outs:
+                copy.start()
         if t >= 1:
             stage_relay(t - 1)
         if t >= 3:

time: 150 us -> 150 us (level)
  no operation moved by 1% of the time
where the time goes in v5:
time: 150 us
  Pallas kernels  149 us (99%)
    pallas_call x1, Pallas kernels, body(): pl.pallas_call(kernel, out_shape=(shape(FEAT, COLS), shape(FEAT, COLS), s...  143 us
    pallas_call x1, Pallas kernels, body(): pl.pallas_call(finish, in_specs=[hbm] * 5, out_specs=(hbm,) * 5, out_shap...  5.95 us

profile of v5, /device:TPU:8, one launch (start us, length us, event | category | flops | bytes accessed | tf_op | source)
XLA Modules:
  0.0 150.0 jit_solution(5068976084065334596)
XLA Ops:
  0.6 143.4 %update.1 = (f32[288,3072]{1,0:T(8,128)}, f32[288,3072]{1,0:T(8,128)}, f32[24,3072]{1,0:T(8,128)}, f32[288]{0:T(512)}, f32[1,3072]{1,0:T(1,128)}) custom-call(bf16[192,3072]{1,0:T(8,128)(2,1)} %cot_hbm.1, bf16[192,2304]{1,0:T(8,128)(2,1)} %act_hbm.1, bf16[192,2304]{1,0:T(8,128)(2,1)} %nxt_hbm.1, f32[288,3072]{1,0:T(8,128)} %w_hbm.1, f32[144,128]{1,0:T(8,128)} %bitcast.3, ...), custom_call_target="tpu_custom_call" | custom-call | flops 5435817984 | bytes 16000000 | tf_op jit(solution)/shard_map/update/pallas_call | solution.py:642
  144.1 5.9 %finish.1 = (f32[288,3072]{1,0:T(8,128)}, f32[288,3072]{1,0:T(8,128)}, f32[24,3072]{1,0:T(8,128)}, f32[288]{0:T(512)}, f32[1,3072]{1,0:T(1,128)}) custom-call(f32[288,3072]{1,0:T(8,128)} %get-tuple-element.15.refs_0_, f32[288,3072]{1,0:T(8,128)} %get-tuple-element.16.refs_1_, f32[24,3072]{1,0:T(8,128)} %get-tuple-element.17.refs_2_, ...), custom_call_target="tpu_custom_call" | custom-call | bytes 14155776 | tf_op jit(solution)/shard_map/finish/pallas_call | solution.py:705
